TPU v7x, 32 devices: a whole 2x2x4 slice. The times are simulated.
32 devices in a mesh: lon: 8 (over y, x, core), lat: 4 (over z).
Axes of the slice: x: 2, y: 2, z: 4, core: 2. Of those that a mesh axis runs over, the one named last changes fastest.
Arguments:
- atmosphere: bfloat16 [128, 512, 256], P('lat', 'lon'), may hold values from -6 to 6
- conv_weight: float32 [7, 7, 256], replicated, may hold values from -0.875 to 0.875
- atm_gain: float32 [256], replicated, may hold values from 0.1 to 1.9
- atm_up: bfloat16 [256, 1024], replicated, may hold values from -0.375 to 0.375
- atm_down: bfloat16 [1024, 256], replicated, may hold values from -0.1875 to 0.1875
- flux_weight: bfloat16 [256, 256], replicated, may hold values from -0.375 to 0.375
- land_mask: int32 [128, 512], P('lat', 'lon'), may hold values from 0 to 1, as said below
- tile_owner: int32 [4, 8, 32], P('lat', 'lon'), may hold values from 0 to 31, as said below
- ocean_state: bfloat16 [32, 32, 2, 64, 256], P(('lat', 'lon')), may hold values from -6 to 6
- ocn_gain: float32 [256], replicated, may hold values from 0.1 to 1.9
- ocn_up: bfloat16 [256, 1024], replicated, may hold values from -0.375 to 0.375
- ocn_down: bfloat16 [1024, 256], replicated, may hold values from -0.1875 to 0.1875
Outputs:
- atm_out: bfloat16 [128, 512, 256], P('lat', 'lon')
- ocean_out: bfloat16 [32, 32, 2, 64, 256], P(('lat', 'lon'))
Inputs may be any that keep to these rules, and one draw needn't show every extreme that they name: `tile_owner`: each entry is the index along lat+lon (lat slowest) of the device that owns the tile. No device owns more than 2 tiles of one device's block, and one device owns exactly 2 tiles of every device's block. `land_mask`: no bound on the number of ocean cells of a tile or of a device may be relied on.
All inputs are finite; a program needn't handle non-finite values.
Results may differ from a plain program's by a relative error of at most 0.0056.
Values may be sent and summed in bfloat16 or wider, within the bound.
No kernel may reach another device: no remote copies, remote signals or barrier semaphores. Data moves between devices by JAX's collectives and lax.ppermute only.
A program may use at most 64 MiB of HBM per device.

v0:
```python
import functools

import jax
import jax.numpy as jnp
from jax import lax
from jax.experimental import pallas as pl
from jax.experimental.pallas import tpu as pltpu
from jax.sharding import PartitionSpec as P

LANES = 128
SENDS = 8
RIM = 8
SIDE = 16
VMEM_BYTES = 48 << 20
F32, BF16 = jnp.float32, jnp.bfloat16
ANY = pl.BlockSpec(memory_space=pl.ANY)
IN_VMEM = pl.BlockSpec(memory_space=pltpu.VMEM)


def hbm(x):
    return pltpu.with_memory_space_constraint(x, pltpu.HBM)


def vmem(x):
    return pltpu.with_memory_space_constraint(x, pltpu.VMEM)


def dot(a, b):
    return jnp.dot(a, b, preferred_element_type=F32)


def iota(shape, dim):
    return lax.broadcasted_iota(jnp.int32, shape, dim)


def spread_weights(w_ref, wb, width):
    for h in range(wb.shape[0]):
        for p in range(width):
            for q in range(width):
                row = w_ref[p, q : q + 1, h * LANES : (h + 1) * LANES]
                wb[h, p * width + q] = jnp.broadcast_to(row, (8, LANES))


PRODUCTS = (
    ((0,), (4,)),
    ((1,), (5,)),
    ((0, 1), (4, 5)),
    ((0, 2), (4, 6)),
    ((1, 3), (5,)),
    ((0, 1, 2, 3), (4, 5, 6)),
    ((2,), (6,)),
    ((3,),),
    ((2, 3), (6,)),
)
WIDTH = 7
MARGIN = WIDTH // 2
TAPS = sum(len(p) for p in PRODUCTS)


def spread_products(w_ref, wb):
    for h in range(wb.shape[0]):
        at = 0
        for product in PRODUCTS:
            for q in range(WIDTH):
                for tap in product:
                    row = None
                    for p in tap:
                        one = w_ref[p, q : q + 1, h * LANES : (h + 1) * LANES]
                        row = one if row is None else row + one
                    wb[h, at] = jnp.broadcast_to(row, (8, LANES))
                    at += 1


def combine_rows(get, put, rows):
    blank = jnp.zeros_like(get(0))
    seen = {}

    def row(r):
        if r < 0 or r >= rows:
            return blank
        if r not in seen:
            seen[r] = get(r)
        return seen[r]

    for m in range(rows // 4 + 1):
        x = [row(4 * m + a - MARGIN) for a in range(WIDTH)]
        d0, d1, d2 = x[0] - x[2], x[1] - x[3], x[2] - x[4]
        e1, e2 = x[5] - x[3], x[6] - x[4]
        values = (d0 - d1, d2 - d1, d1, x[2] - x[3], x[4] - x[3], x[3], -d2 - e1, e2 - e1, e1)
        for k, value in enumerate(values):
            put(k, m, value)


GIVES = ((0,), (1,), (0, 1), (0, 2), (1, 3), (0, 1, 2, 3), (2,), (3,), (2, 3))


def filter_rows(read, wb, h, count):
    out = [None] * (4 * count)
    at = 0
    for k, product in enumerate(PRODUCTS):
        acc = [None] * count
        for q in range(WIDTH):
            window = [read(k, m, q) for m in range(count + len(product) - 1)]
            for t in range(len(product)):
                w = wb[h, at]
                at += 1
                for m in range(count):
                    term = window[m + t] * w
                    acc[m] = term if acc[m] is None else acc[m] + term
        for m in range(count):
            for i in GIVES[k]:
                before = out[4 * m + i]
                out[4 * m + i] = acc[m] if before is None else before + acc[m]
    return out


def edges_kernel(x_ref, w_ref, own_ref, kept_ref, first_ref, last_ref, sems):
    cols = own_ref.shape[1]
    copies = [
        pltpu.make_async_copy(x_ref, own_ref, sems.at[0]),
        pltpu.make_async_copy(w_ref, kept_ref, sems.at[1]),
    ]
    for copy in copies:
        copy.start()
    for copy in copies:
        copy.wait()
    first_ref[...] = own_ref[:, 0:RIM]
    last_ref[...] = own_ref[:, cols - RIM :]


def edges(atmosphere, conv_weight):
    rows, _, channels = atmosphere.shape
    return pl.pallas_call(
        edges_kernel,
        out_shape=[
            pltpu.VMEM(atmosphere.shape, BF16),
            pltpu.VMEM(conv_weight.shape, F32),
            pltpu.VMEM((rows, RIM, channels), BF16),
            pltpu.VMEM((rows, RIM, channels), BF16),
        ],
        in_specs=[ANY, ANY],
        out_specs=[IN_VMEM] * 4,
        scratch_shapes=[pltpu.SemaphoreType.DMA((2,))],
        compiler_params=pltpu.CompilerParams(vmem_limit_bytes=VMEM_BYTES),
        name="edges",
    )(hbm(atmosphere), hbm(conv_weight))


GROUP = 8


def inner_kernel(own_ref, w_ref, mixed_ref, wb, fs):
    rows, cols, channels = own_ref.shape
    spread_products(w_ref, wb)
    halves = channels // LANES
    first = SIDE - RIM
    for h in range(halves):
        part = slice(h * LANES, (h + 1) * LANES)

        def prepare(c, carry):
            c0 = pl.multiple_of(c * 16, 16)

            def put(k, m, value):
                fs[h, k, m, pl.ds(c0, 16)] = value

            combine_rows(lambda r: own_ref[r, pl.ds(c0 + first, 16), part].astype(F32), put, rows)
            return carry

        lax.fori_loop(0, fs.shape[3] // 16, prepare, 0)
    blocks = (cols - 2 * SIDE) // 8

    def body(step, carry):
        m0 = (step // blocks) * GROUP
        c0 = pl.multiple_of((step % blocks) * 8, 8)
        for h in range(halves):
            out = filter_rows(
                lambda k, m, q: fs[h, k, m0 + m, pl.ds(c0 + (RIM - MARGIN + q), 8)], wb, h, GROUP
            )
            for i, value in enumerate(out):
                mixed_ref[h, m0 * 4 + i, pl.ds(c0 + SIDE, 8)] = value
        return carry

    lax.fori_loop(0, (rows // 4 // GROUP) * blocks, body, 0)


def conv_inner(own, conv_weight):
    rows, cols, channels = own.shape
    halves = channels // LANES
    return pl.pallas_call(
        inner_kernel,
        out_shape=[
            pltpu.VMEM((halves, rows, cols, LANES), F32),
            pltpu.VMEM((halves, WIDTH * TAPS, 8, LANES), F32),
        ],
        in_specs=[IN_VMEM, IN_VMEM],
        out_specs=[IN_VMEM, IN_VMEM],
        scratch_shapes=[
            pltpu.VMEM((halves, len(PRODUCTS), rows // 4 + 1, cols - 2 * (SIDE - RIM), LANES), F32),
        ],
        compiler_params=pltpu.CompilerParams(vmem_limit_bytes=VMEM_BYTES),
        cost_estimate=pl.CostEstimate(
            flops=2 * rows * cols * channels * WIDTH * WIDTH, bytes_accessed=6 * rows * cols * channels, transcendentals=0
        ),
        name="conv_inner",
    )(vmem(own), vmem(conv_weight))


def outer_kernel(mixed_in, own_ref, left_ref, right_ref, wb, *refs, count):
    far, mixed_ref, near = refs[:count], refs[count], refs[count + 1 : 2 * count + 1]
    fs, sems = refs[2 * count + 1 :]
    fetches = [pltpu.make_async_copy(f, n, sems.at[i]) for i, (f, n) in enumerate(zip(far, near))]
    for fetch in fetches:
        fetch.start()
    rows, cols, channels = own_ref.shape
    halves = channels // LANES
    blocks = SIDE // 8
    for side in range(2):
        rim, edge = (left_ref, 0) if side == 0 else (right_ref, SIDE + RIM)
        body_at, own_at = (RIM, 0) if side == 0 else (0, cols - SIDE - RIM)
        for h in range(halves):
            part = slice(h * LANES, (h + 1) * LANES)

            def put_rim(k, m, value):
                fs[k, m, edge : edge + RIM] = value

            combine_rows(lambda r: rim[r, :, part].astype(F32), put_rim, rows)

            def prepare(c, carry):
                c0 = pl.multiple_of(c * 8, 8)

                def put(k, m, value):
                    fs[k, m, pl.ds(c0 + body_at, 8)] = value

                combine_rows(lambda r: own_ref[r, pl.ds(c0 + own_at, 8), part].astype(F32), put, rows)
                return carry

            lax.fori_loop(0, blocks + 1, prepare, 0)

            def body(step, carry):
                m0 = (step // blocks) * GROUP
                c0 = pl.multiple_of((step % blocks) * 8, 8)
                out = filter_rows(
                    lambda k, m, q: fs[k, m0 + m, pl.ds(c0 + (RIM - MARGIN + q), 8)], wb, h, GROUP
                )
                for i, value in enumerate(out):
                    mixed_ref[h, m0 * 4 + i, pl.ds(c0 + side * (cols - SIDE), 8)] = value
                return carry

            lax.fori_loop(0, (rows // 4 // GROUP) * blocks, body, 0)
    for fetch in fetches:
        fetch.wait()


def conv_outer(mixed, own, left, right, products, weights):
    rows, cols, channels = own.shape
    halves = channels // LANES
    count = len(weights)
    return pl.pallas_call(
        functools.partial(outer_kernel, count=count),
        out_shape=[pltpu.VMEM(mixed.shape, F32)] + [pltpu.VMEM(w.shape, w.dtype) for w in weights],
        in_specs=[IN_VMEM] * 5 + [ANY] * count,
        out_specs=[IN_VMEM] * (count + 1),
        input_output_aliases={0: 0},
        scratch_shapes=[
            pltpu.VMEM((len(PRODUCTS), rows // 4 + 1, SIDE + 2 * RIM, LANES), F32),
            pltpu.SemaphoreType.DMA((count,)),
        ],
        compiler_params=pltpu.CompilerParams(vmem_limit_bytes=VMEM_BYTES),
        cost_estimate=pl.CostEstimate(
            flops=4 * rows * RIM * channels * WIDTH * WIDTH, bytes_accessed=12 * rows * RIM * channels, transcendentals=0
        ),
        name="conv_outer",
    )(vmem(mixed), vmem(own), vmem(left), vmem(right), vmem(products), *[hbm(w) for w in weights])


def widen_kernel(own_ref, left_ref, right_ref, mixed_ref, up_ref, down_ref):
    margin = up_ref.shape[0]
    rows, cols, _ = own_ref.shape
    for out, at in ((up_ref, 0), (down_ref, rows - margin)):
        out[:, 0:RIM] = left_ref[at : at + margin]
        out[:, RIM : RIM + cols] = own_ref[at : at + margin]
        out[:, RIM + cols :] = right_ref[at : at + margin]


def widen(own, left, right, mixed, margin):
    rows, cols, channels = own.shape
    return pl.pallas_call(
        widen_kernel,
        out_shape=[pltpu.VMEM((margin, cols + 2 * RIM, channels), BF16)] * 2,
        in_specs=[IN_VMEM] * 4,
        out_specs=[IN_VMEM] * 2,
        compiler_params=pltpu.CompilerParams(vmem_limit_bytes=VMEM_BYTES),
        name="widen_rows",
    )(vmem(own), vmem(left), vmem(right), vmem(mixed))


def normalize(values, gain):
    average = jnp.mean(values, axis=-1, keepdims=True)
    centred = values - average
    spread = jnp.mean(centred * centred, axis=-1, keepdims=True)
    return (centred * lax.rsqrt(spread + 1e-06) * gain).astype(BF16)


def mixer(normed, up_ref, down_ref, chunk=256):
    c0 = 0.7978845608028654
    c1 = c0 * 0.044715
    total = None
    for j in range(0, up_ref.shape[1], chunk):
        x = dot(normed, up_ref[:, j : j + chunk])
        gate = jnp.tanh(x * (c0 + c1 * (x * x)))
        hidden = (x + x * gate).astype(BF16)
        part = dot(hidden, down_ref[j : j + chunk, :])
        total = part if total is None else total + part
    return 0.5 * total


def atmosphere_kernel(
    tiles, capacity, tile, owner_sm, mixed_in, atm_ref, top_ref, bottom_ref, w_ref, gain_ref, up_ref, down_ref,
    flux_ref, owner_ref, mask_ref, out_ref, send_ref, rest_ref, mark_ref, mixed_ref,
    wb, strip, fluxes, order_sm, meta, places, new_out, packets, rest, out_sems, send_sems, rest_sems,
):
    rows, cols, channels = atm_ref.shape
    width = w_ref.shape[0]
    margin = width // 2
    halves = channels // LANES
    peers, packed, _ = send_ref.shape
    pair = capacity * tile

    def lanes(h):
        return slice(h * LANES, (h + 1) * LANES)

    spread_weights(w_ref, wb, width)

    def latitude(rows_ref, pairs):
        for h in range(halves):
            strip[h] = rows_ref[:, :, lanes(h)].astype(F32)

        def body(c, carry):
            c0 = pl.multiple_of(c * 8, 8)
            for h in range(halves):
                for i, taps in pairs:
                    acc = mixed_ref[h, i, pl.ds(c0, 8)]
                    for row, p in taps:
                        for q in range(width):
                            acc += strip[h, row, pl.ds(c0 + (RIM - margin + q), 8)] * wb[h, p * width + q]
                    mixed_ref[h, i, pl.ds(c0, 8)] = acc
            return carry

        lax.fori_loop(0, cols // 8, body, 0)

    latitude(top_ref, [(i, [(i + p, p) for p in range(margin - i)]) for i in range(margin)])
    latitude(
        bottom_ref,
        [
            (rows - margin + i, [(i - e, width - 1 - e) for e in range(i + 1)])
            for i in range(margin)
        ],
    )

    block = 16
    cells = block * cols

    def leave(step):
        part = pl.ds(step * block, block)
        return pltpu.make_async_copy(new_out.at[part], out_ref.at[part], out_sems.at[step])

    def mix(step, carry):
        r0 = step * block
        parts = [mixed_ref[h, pl.ds(r0, block)].reshape(cells, LANES) for h in range(halves)]
        normed = normalize(jnp.concatenate(parts, axis=1), gain_ref[...])
        branch = mixer(normed, up_ref, down_ref)
        new = (atm_ref[pl.ds(r0, block)].reshape(cells, channels).astype(F32) + branch).astype(BF16)
        new_out[pl.ds(r0, block)] = new.reshape(block, cols, channels)
        leave(step).start()
        fluxes[pl.ds(pl.multiple_of(step * cells, cells), cells), :] = dot(new, flux_ref[...]).astype(BF16)
        return carry

    lax.fori_loop(0, rows // block, mix, 0)

    member = (owner_ref[...] == iota((peers, tiles), 0)).astype(F32)
    before = (iota((tiles, tiles), 0) < iota((tiles, tiles), 1)).astype(BF16)
    rank = dot(member.astype(BF16), before)
    bits = jnp.zeros((peers, LANES), F32)
    flags = jnp.zeros((peers, LANES), F32)
    lane = iota((peers, LANES), 1)
    for r in range(capacity):
        chosen = jnp.where(rank == float(r), member, 0.0)
        at = (iota((tile, LANES), 1) == iota((tile, LANES), 0) + r * tile).astype(BF16)
        shifted = dot(mask_ref[...].astype(F32).astype(BF16), at).astype(BF16)
        bits += dot(chosen.astype(BF16), shifted)
        flags += jnp.where(lane == r, jnp.sum(chosen, axis=1, keepdims=True), 0.0)
    over = jnp.max(jnp.sum(bits, axis=1, keepdims=True), axis=0, keepdims=True) > float(packed - 1)
    flags += jnp.where((lane == capacity) & over, 1.0, 0.0)
    meta[:, 0:LANES] = bits
    meta[:, LANES:] = flags
    ahead = jnp.where(
        iota((LANES, LANES), 0) < iota((LANES, LANES), 1),
        1.0,
        jnp.where(iota((LANES, LANES), 0) == iota((LANES, LANES), 1), 1000.0, 0.0),
    ).astype(BF16)
    places[...] = (dot(bits.astype(BF16), ahead) - 999.0).astype(jnp.int32)

    def clear(o, carry):
        for r in range(capacity):
            order_sm[o * capacity + r] = 0
        order_sm[peers * capacity + o] = 0
        return carry

    lax.fori_loop(0, peers, clear, 0)

    def count(t, carry):
        o = owner_sm[t]
        r = order_sm[peers * capacity + o]
        order_sm[o * capacity + r] = t
        order_sm[peers * capacity + o] = r + 1
        return carry

    lax.fori_loop(0, tiles, count, 0)
    order = iota((packed + rest_ref.shape[1], LANES), 0)
    top_row = iota((packed, channels), 0) == 0
    group = peers // SENDS

    def send(i):
        part = pl.ds(i * group, group)
        return (
            pltpu.make_async_copy(packets.at[part], send_ref.at[part], send_sems.at[i]),
            pltpu.make_async_copy(rest.at[part], rest_ref.at[part], rest_sems.at[i]),
        )

    def pack(i, carry):
        for k in range(group):
            o = i * group + k
            held = [
                fluxes[pl.ds(pl.multiple_of(order_sm[o * capacity + r] * tile, tile), tile), :]
                for r in range(capacity)
            ]
            pick = jnp.where(order == places[pl.ds(o, 1), :], 1.0, 0.0).astype(BF16)
            packet = dot(pick[:, 0:pair], jnp.concatenate(held, axis=0))
            packets[o] = jnp.where(top_row, meta[pl.ds(o, 1), :], packet[0:packed]).astype(BF16)
            rest[o] = packet[packed:].astype(BF16)
        for copy in send(i):
            copy.start()
        return carry

    lax.fori_loop(0, SENDS, pack, 0)
    mark_ref[...] = jnp.zeros(mark_ref.shape, F32)
    for step in range(rows // block):
        leave(step).wait()
    for i in range(SENDS):
        for copy in send(i):
            copy.wait()


def atmosphere_step(
    mixed, own, top, bottom, conv_weight, gain, w_up, w_down, w_flux, owners, mask, peers, capacity, tile, packed
):
    rows, cols, channels = own.shape
    tiles = owners.shape[0]
    width = conv_weight.shape[0]
    margin = width // 2
    halves = channels // LANES
    hidden = w_up.shape[1]
    cells = rows * cols
    remaining = -(-(capacity * tile + 1 - packed) // 16) * 16
    in_smem = pl.BlockSpec(memory_space=pltpu.SMEM)
    return pl.pallas_call(
        functools.partial(atmosphere_kernel, tiles, capacity, tile),
        out_shape=[
            jax.ShapeDtypeStruct((rows, cols, channels), BF16),
            jax.ShapeDtypeStruct((peers, packed, channels), BF16),
            jax.ShapeDtypeStruct((peers, remaining, channels), BF16),
            jax.ShapeDtypeStruct((8, LANES), F32),
            pltpu.VMEM(mixed.shape, F32),
        ],
        in_specs=[in_smem] + [IN_VMEM] * 11,
        out_specs=[ANY, ANY, ANY, IN_VMEM, IN_VMEM],
        input_output_aliases={1: 4},
        scratch_shapes=[
            pltpu.VMEM((halves, width * width, 8, LANES), F32),
            pltpu.VMEM((halves, margin, cols + 2 * RIM, LANES), F32),
            pltpu.VMEM((cells, channels), BF16),
            pltpu.SMEM((peers * (capacity + 1),), jnp.int32),
            pltpu.VMEM((peers, 2 * LANES), F32),
            pltpu.VMEM((peers, LANES), jnp.int32),
            pltpu.VMEM((rows, cols, channels), BF16),
            pltpu.VMEM((peers, packed, channels), BF16),
            pltpu.VMEM((peers, remaining, channels), BF16),
            pltpu.SemaphoreType.DMA((rows,)),
            pltpu.SemaphoreType.DMA((SENDS,)),
            pltpu.SemaphoreType.DMA((SENDS,)),
        ],
        compiler_params=pltpu.CompilerParams(vmem_limit_bytes=VMEM_BYTES),
        cost_estimate=pl.CostEstimate(
            flops=2 * cells * channels * (2 * hidden + channels), bytes_accessed=12 * cells * channels,
            transcendentals=cells * hidden,
        ),
        name="atmosphere",
    )(
        owners, vmem(mixed), vmem(own), vmem(top), vmem(bottom), vmem(conv_weight), gain.reshape(1, -1), vmem(w_up),
        vmem(w_down), vmem(w_flux), owners.reshape(1, -1), mask,
    )


def fetch_kernel(mark_ref, *refs):
    count = (len(refs) - 1) // 2
    copies = [
        pltpu.make_async_copy(refs[i], refs[count + i], refs[-1].at[i]) for i in range(count)
    ]
    for copy in copies:
        copy.start()
    for copy in copies:
        copy.wait()


def fetch(mark, arrays):
    return pl.pallas_call(
        fetch_kernel,
        out_shape=[pltpu.VMEM(x.shape, x.dtype) for x in arrays],
        in_specs=[ANY] * (len(arrays) + 1),
        out_specs=[IN_VMEM] * len(arrays),
        scratch_shapes=[pltpu.SemaphoreType.DMA((len(arrays),))],
        compiler_params=pltpu.CompilerParams(vmem_limit_bytes=VMEM_BYTES),
        name="fetch",
    )(mark, *[hbm(x) for x in arrays])


def ocean_kernel(
    capacity, chain, state_ref, packet_hbm, gain_ref, up_ref, down_ref, out_hbm, over_ref, packet_ref, out_ref,
    in_sems, out_sems,
):
    peers, pair, channels = state_ref.shape
    packed = packet_ref.shape[1]
    tile = pair // capacity
    chains = peers // chain

    def arrive(i):
        part = pl.ds(i * chain, chain)
        return pltpu.make_async_copy(packet_hbm.at[part], packet_ref.at[part], in_sems.at[i])

    def leave(i):
        part = pl.ds(i * chain, chain)
        return pltpu.make_async_copy(out_ref.at[part], out_hbm.at[part], out_sems.at[i])

    for i in range(chains):
        arrive(i).start()
    ahead = jnp.where(
        iota((pair, LANES), 1) < iota((pair, LANES), 0),
        1.0,
        jnp.where(iota((pair, LANES), 1) == iota((pair, LANES), 0), 1000.0, 0.0),
    ).astype(BF16)
    order = iota((pair, packed), 1)

    def mix(i, over):
        arrive(i).wait()
        first = i * chain
        head = jnp.concatenate([packet_ref[first + g, 0:1, :] for g in range(chain)], axis=0)
        place = lax.dot_general(
            ahead, head[:, 0:LANES], (((1,), (1,)), ((), ())), preferred_element_type=F32
        )
        place = (place - 999.0).astype(jnp.int32)
        flags = head[:, LANES:].astype(F32)
        states = []
        for g in range(chain):
            pick = jnp.where(order == place[:, g : g + 1], 1.0, 0.0).astype(BF16)
            states.append(state_ref[first + g].astype(F32) + dot(pick, packet_ref[first + g]))
        states = jnp.concatenate(states, axis=0)
        result = states + mixer(normalize(states, gain_ref[...]), up_ref, down_ref)
        for g in range(chain):
            for r in range(capacity):
                used = flags[g : g + 1, r : r + 1] > 0.0
                at = g * pair + r * tile
                part = jnp.where(used, result[at : at + tile], 0.0)
                out_ref[first + g, r * tile : (r + 1) * tile, :] = part.astype(BF16)
        leave(i).start()
        return jnp.maximum(over, jnp.max(flags[:, capacity : capacity + 1], axis=0, keepdims=True))

    over = lax.fori_loop(0, chains, mix, jnp.zeros((1, 1), F32))
    over_ref[0, 0] = jnp.max(over)
    for i in range(chains):
        leave(i).wait()


def ocean_step(state, packets, gain, w_up, w_down, capacity):
    peers, pair, channels = state.shape
    packed = packets.shape[1]
    hidden = w_up.shape[1]
    chain = min(peers, 1024 // pair)
    chains = peers // chain
    cells = peers * pair
    return pl.pallas_call(
        functools.partial(ocean_kernel, capacity, chain),
        out_shape=[
            jax.ShapeDtypeStruct((peers, pair, channels), BF16),
            jax.ShapeDtypeStruct((1, 1), F32),
        ],
        in_specs=[IN_VMEM, ANY, IN_VMEM, IN_VMEM, IN_VMEM],
        out_specs=[ANY, pl.BlockSpec(memory_space=pltpu.SMEM)],
        scratch_shapes=[
            pltpu.VMEM((peers, packed, channels), BF16),
            pltpu.VMEM((peers, pair, channels), BF16),
            pltpu.SemaphoreType.DMA((chains,)),
            pltpu.SemaphoreType.DMA((chains,)),
        ],
        compiler_params=pltpu.CompilerParams(vmem_limit_bytes=VMEM_BYTES),
        cost_estimate=pl.CostEstimate(
            flops=4 * cells * channels * hidden, bytes_accessed=6 * cells * channels, transcendentals=cells * hidden
        ),
        name="ocean",
    )(vmem(state), hbm(packets), gain, vmem(w_up), vmem(w_down))


def per_device(
    atmosphere,
    conv_weight,
    atm_gain,
    atm_up,
    atm_down,
    flux_weight,
    land_mask,
    tile_owner,
    ocean_state,
    ocn_gain,
    ocn_up,
    ocn_down,
):
    margin = conv_weight.shape[0] // 2
    channels = atmosphere.shape[2]
    _, peers, capacity, tile, _ = ocean_state.shape
    pair = capacity * tile
    packed = -(-(pair * 13 // 16) // 8) * 8
    n_lon, n_lat = lax.axis_size("lon"), lax.axis_size("lat")
    owners = tile_owner.reshape(-1)
    state = ocean_state.reshape(peers, pair, channels)

    around = [(i, (i + 1) % n_lon) for i in range(n_lon)]
    own, conv_weight, first, last = edges(atmosphere, conv_weight)
    left = lax.ppermute(last, "lon", around)
    right = lax.ppermute(first, "lon", [(j, i) for i, j in around])
    mixed, products = conv_inner(own, conv_weight)
    up, down = widen(own, left, right, mixed, margin)
    north = [(i, i + 1) for i in range(n_lat - 1)]
    top = lax.ppermute(down, "lat", north)
    bottom = lax.ppermute(up, "lat", [(j, i) for i, j in north])
    mixed, w_up, w_down, w_flux = conv_outer(
        mixed, own, left, right, products, (atm_up, atm_down, flux_weight)
    )
    atm_out, packets, rest, mark, _ = atmosphere_step(
        mixed, own, top, bottom, conv_weight, atm_gain, w_up, w_down, w_flux, owners,
        land_mask.reshape(owners.shape[0], tile), peers, capacity, tile, packed,
    )

    def exchange(x):
        return lax.all_to_all(x, ("lat", "lon"), split_axis=0, concat_axis=0, tiled=True)

    arrived = exchange(packets)
    near = fetch(mark, (state, ocn_gain.reshape(1, -1), ocn_up, ocn_down))
    ocean_out, over = ocean_step(near[0], arrived, *near[1:], capacity)

    def with_rest(packed_out):
        everything = jnp.concatenate([arrived, exchange(rest)], axis=1)
        return ocean_step(near[0], everything, *near[1:], capacity)[0]

    ocean_out = lax.cond(over[0, 0] > 0, with_rest, lambda packed_out: packed_out, ocean_out)
    return atm_out, ocean_out.reshape(ocean_state.shape)


def solution(mesh):
    placed = (
        P("lat", "lon", None),
        P(),
        P(),
        P(),
        P(),
        P(),
        P("lat", "lon"),
        P("lat", "lon", None),
        P(("lat", "lon"), None, None, None, None),
        P(),
        P(),
        P(),
    )
    return jax.shard_map(
        per_device,
        mesh=mesh,
        in_specs=placed,
        out_specs=(P("lat", "lon", None), P(("lat", "lon"), None, None, None, None)),
        check_vma=False,
    )
```

profile of v0, /device:TPU:0, one launch (start us, length us, event | category | flops | bytes accessed | tf_op | source)
XLA Modules:
  0.0 88.7 jit_solution(16113393909323770500)
XLA Ops:
  0.6 1.3 %edges.1 = (bf16[32,64,256]{2,1,0:T(8,128)(2,1)S(1)}, f32[7,7,256]{2,1,0:T(8,128)S(1)}, bf16[32,8,256]{2,1,0:T(8,128)(2,1)S(1)}, bf16[32,8,256]{2,1,0:T(8,128)(2,1)S(1)}) custom-call(bf16[32,64,256]{2,1,0:T(8,128)(2,1)} %x_ref.1, f32[7,7,256]{2,1,0:T(8,128)} %w_ref.1), custom_call_target="tpu_custom_call" | custom-call | tf_op jit(solution)/shard_map/edges/pallas_call | solution.py:133
  1.9 0.5 collective-permute-start
  2.4 2.9 %collective-permute-start.1 = (bf16[32,8,256]{2,1,0:T(8,128)(2,1)S(1)}, bf16[32,8,256]{2,1,0:T(8,128)(2,1)S(1)}, u32[]{:S(2)}, u32[]{:S(2)}) collective-permute-start(bf16[32,8,256]{2,1,0:T(8,128)(2,1)S(1)} %get-tuple-element.57), channel_id=1, source_target_pairs={{4,0},{8,4},{12,8},{16,12},{20,16},{24,20},{28,24},{0,28},{5,1},{9... | collective-permute-start | bytes 393224 | tf_op jit(solution)/shard_map/ppermute | solution.py:638
  5.4 4.4 %conv_inner.1 = (f32[2,32,64,128]{3,2,1,0:T(8,128)S(1)}, f32[2,119,8,128]{3,2,1,0:T(8,128)S(1)}) custom-call(bf16[32,64,256]{2,1,0:T(8,128)(2,1)S(1)} %get-tuple-element.53.own_ref.atm_ref, f32[7,7,256]{2,1,0:T(8,128)S(1)} %get-tuple-element.54.w_ref), custom_call_target="tpu_custom_call" | custom-call | flops 51380224 | bytes 3145728 | tf_op jit(solution)/shard_map/conv_inner/pallas_call | solution.py:189
  9.8 0.0 collective-permute-done.left_ref
  9.8 0.0 collective-permute-done.1.right_ref
  9.8 4.2 %collective-permute-start.2 = (bf16[3,80,256]{2,1,0:T(8,128)(2,1)S(1)}, bf16[3,80,256]{2,1,0:T(8,128)(2,1)S(1)}, u32[]{:S(2)}, u32[]{:S(2)}) collective-permute-start(bf16[3,80,256]{2,1,0:T(8,128)(2,1)S(1)} %get-tuple-element.60), channel_id=1, source_target_pairs={{0,1},{1,2},{2,3},{4,5},{5,6},{6,7},{8,9},{9,10},{10,11},{12,13},{... | collective-permute-start | bytes 368648 | tf_op jit(solution)/shard_map/ppermute | solution.py:642
  14.0 1.3 %collective-permute-start.3 = (bf16[3,80,256]{2,1,0:T(8,128)(2,1)S(1)}, bf16[3,80,256]{2,1,0:T(8,128)(2,1)S(1)}, u32[]{:S(2)}, u32[]{:S(2)}) collective-permute-start(bf16[3,80,256]{2,1,0:T(8,128)(2,1)S(1)} %get-tuple-element.61), channel_id=1, source_target_pairs={{1,0},{2,1},{3,2},{5,4},{6,5},{7,6},{9,8},{10,9},{11,10},{13,12},{... | collective-permute-start | bytes 368648 | tf_op jit(solution)/shard_map/ppermute | solution.py:643
  15.3 0.0 copy-start
  15.3 0.0 copy-start.1
  15.3 0.0 copy-start.2
  15.3 5.3 %conv_outer.1 = (f32[2,32,64,128]{3,2,1,0:T(8,128)S(1)}, bf16[256,1024]{1,0:T(8,128)(2,1)S(1)}, bf16[1024,256]{1,0:T(8,128)(2,1)S(1)}, bf16[256,256]{1,0:T(8,128)(2,1)S(1)}) custom-call(f32[2,32,64,128]{3,2,1,0:T(8,128)S(1)} %get-tuple-element.55.mixed_in.mixed_ref, ...), custom_call_target="tpu_custom_call", output_to_operand_aliasing={{0}: (0, {})} | custom-call | flops 12845056 | bytes 786432 | tf_op jit(solution)/shard_map/conv_outer/pallas_call | solution.py:258
  20.6 0.0 collective-permute-done.2.top_ref
  20.6 0.1 collective-permute-done.3.bottom_ref
  20.8 0.0 copy-done
  20.8 0.0 copy-done.1
  20.8 0.0 copy-done.2
  20.8 9.2 %atmosphere.1 = (bf16[32,64,256]{2,1,0:T(8,128)(2,1)}, bf16[32,104,256]{2,1,0:T(8,128)(2,1)}, bf16[32,32,256]{2,1,0:T(8,128)(2,1)}, f32[8,128]{1,0:T(8,128)S(1)}, f32[2,32,64,128]{3,2,1,0:T(8,128)S(1)}) custom-call(s32[32]{0:T(128)S(1)} %bitcast.8, f32[2,32,64,128]{3,2,1,0:T(8,128)S(1)} %get-tuple-element.59.mixed_in, ...), custom_call_target="tpu_custom_call", output_to_operand_aliasing={{4}: (1, {})} | custom-call | flops 2415919104 | bytes 6291456 | tf_op jit(solution)/shard_map/atmosphere/pallas_call | solution.py:466
  30.0 6.0 %all-to-all-start.1 = ((bf16[32,104,256]{2,1,0:T(8,128)(2,1)}), bf16[32,104,256]{2,1,0:T(8,128)(2,1)}, u32[]{:S(2)}, u32[]{:S(2)}) async-start(bf16[32,104,256]{2,1,0:T(8,128)(2,1)} %get-tuple-element.68), calls=%async_computation.1 | async-start | bytes 3407872 | tf_op jit(solution)/shard_map/all_to_all | solution.py:653
  36.1 1.9 %fetch.1 = (bf16[32,128,256]{2,1,0:T(8,128)(2,1)S(1)}, f32[1,256]{1,0:T(1,128)S(1)}, bf16[256,1024]{1,0:T(8,128)(2,1)S(1)}, bf16[1024,256]{1,0:T(8,128)(2,1)S(1)}) custom-call(f32[8,128]{1,0:T(8,128)S(1)} %get-tuple-element.66.mark_ref, bf16[32,128,256]{2,1,0:T(8,128)(2,1)} %bitcast.10, f32[1,256]{1,0:T(1,128)} %bitcast.11, bf16[256,1024]{1,0:T(8,128)(2,1)} %refs_2_.3, ...), custom_call_target="tpu_custom_call" | custom-call | tf_op jit(solution)/shard_map/fetch/pallas_call | solution.py:516
  38.0 38.5 %all-to-all-done.1.packet_hbm = bf16[32,104,256]{2,1,0:T(8,128)(2,1)} async-done(((bf16[32,104,256]{2,1,0:T(8,128)(2,1)}), bf16[32,104,256]{2,1,0:T(8,128)(2,1)}, u32[]{:S(2)}, u32[]{:S(2)}) %all-to-all-start.1) | async-done | bytes 1703968 | tf_op jit(solution)/shard_map/all_to_all | solution.py:653
  76.5 0.0 copy-start.3
  76.5 11.6 %ocean.3 = (bf16[32,128,256]{2,1,0:T(8,128)(2,1)}, f32[1,1]{1,0:T(1,128)}) custom-call(bf16[32,128,256]{2,1,0:T(8,128)(2,1)S(1)} %get-tuple-element.67.state_ref, bf16[32,104,256]{2,1,0:T(8,128)(2,1)} %all-to-all-done.1.packet_hbm, f32[1,256]{1,0:T(1,128)S(1)} %get-tuple-element.69.gain_ref, bf16[256,1024]{1,0:T(8,128)(2,1)S(1)} %get-tuple-element.70.up_ref, ...), custom_call_target="tpu_custom_call" | custom-call | flops 4294967296 | bytes 6291456 | tf_op jit(solution)/shard_map/ocean/pallas_call | solution.py:590
  88.7 0.0 copy-done.3
  (2 shorter events, 0.0 us)
Async XLA Ops:
  1.9 7.8 %collective-permute-start = (bf16[32,8,256]{2,1,0:T(8,128)(2,1)S(1)}, bf16[32,8,256]{2,1,0:T(8,128)(2,1)S(1)}, u32[]{:S(2)}, u32[]{:S(2)}) collective-permute-start(bf16[32,8,256]{2,1,0:T(8,128)(2,1)S(1)} %get-tuple-element.56), channel_id=1, source_target_pairs={{0,4},{4,8},{8,12},{12,16},{16,20},{20,24},{24,28},{28,0},{1,5},{5... | collective-permute-start | bytes 393224 | tf_op jit(solution)/shard_map/ppermute | solution.py:637
  2.4 7.3 %collective-permute-start.1 = (bf16[32,8,256]{2,1,0:T(8,128)(2,1)S(1)}, bf16[32,8,256]{2,1,0:T(8,128)(2,1)S(1)}, u32[]{:S(2)}, u32[]{:S(2)}) collective-permute-start(bf16[32,8,256]{2,1,0:T(8,128)(2,1)S(1)} %get-tuple-element.57), channel_id=1, source_target_pairs={{4,0},{8,4},{12,8},{16,12},{20,16},{24,20},{28,24},{0,28},{5,1},{9... | collective-permute-start | bytes 393224 | tf_op jit(solution)/shard_map/ppermute | solution.py:638
  9.8 10.8 %collective-permute-start.2 = (bf16[3,80,256]{2,1,0:T(8,128)(2,1)S(1)}, bf16[3,80,256]{2,1,0:T(8,128)(2,1)S(1)}, u32[]{:S(2)}, u32[]{:S(2)}) collective-permute-start(bf16[3,80,256]{2,1,0:T(8,128)(2,1)S(1)} %get-tuple-element.60), channel_id=1, source_target_pairs={{0,1},{1,2},{2,3},{4,5},{5,6},{6,7},{8,9},{9,10},{10,11},{12,13},{... | collective-permute-start | bytes 368648 | tf_op jit(solution)/shard_map/ppermute | solution.py:642
  14.0 6.8 %collective-permute-start.3 = (bf16[3,80,256]{2,1,0:T(8,128)(2,1)S(1)}, bf16[3,80,256]{2,1,0:T(8,128)(2,1)S(1)}, u32[]{:S(2)}, u32[]{:S(2)}) collective-permute-start(bf16[3,80,256]{2,1,0:T(8,128)(2,1)S(1)} %get-tuple-element.61), channel_id=1, source_target_pairs={{1,0},{2,1},{3,2},{5,4},{6,5},{7,6},{9,8},{10,9},{11,10},{13,12},{... | collective-permute-start | bytes 368648 | tf_op jit(solution)/shard_map/ppermute | solution.py:643
  15.3 5.5 %copy-start = (s32[32,64]{1,0:T(8,128)S(1)}, s32[32,64]{1,0:T(8,128)}, u32[]{:S(2)}) copy-start(s32[32,64]{1,0:T(8,128)} %mask_ref.1) | copy-start | bytes 24580
  15.3 5.5 %copy-start.1 = (f32[256]{0:T(256)S(1)}, f32[256]{0:T(256)}, u32[]{:S(2)}) copy-start(f32[256]{0:T(256)} %param.16) | copy-start | bytes 3076
  15.3 5.5 %copy-start.2 = (s32[1,1,32]{2,1,0:T(1,128)S(1)}, s32[1,1,32]{2,1,0:T(1,128)}, u32[]{:S(2)}) copy-start(s32[1,1,32]{2,1,0:T(1,128)} %param.21) | copy-start | bytes 388
  30.0 46.5 %all-to-all-start.1 = ((bf16[32,104,256]{2,1,0:T(8,128)(2,1)}), bf16[32,104,256]{2,1,0:T(8,128)(2,1)}, u32[]{:S(2)}, u32[]{:S(2)}) async-start(bf16[32,104,256]{2,1,0:T(8,128)(2,1)} %get-tuple-element.68), calls=%async_computation.1 | async-start | bytes 3407872 | tf_op jit(solution)/shard_map/all_to_all | solution.py:653
  76.5 12.2 %copy-start.3 = (bf16[32,32,256]{2,1,0:T(8,128)(2,1)S(1)}, bf16[32,32,256]{2,1,0:T(8,128)(2,1)}, u32[]{:S(2)}) copy-start(bf16[32,32,256]{2,1,0:T(8,128)(2,1)} %get-tuple-element.74) | copy-start | bytes 1572868
where the time goes:
time: 89 us; the launch traced here: 88.7 us
  waiting for transfers between devices  38.6 us (43%)
  Pallas kernels  33.7 us (38%)
  starting transfers between devices  15 us (17%)
  between operations  1.4 us (2%)
    all_to_all x1, waiting for transfers between devices, exchange(): lax.all_to_all(x, ('lat', 'lon'), split_axis=0, concat_axis=0, tiled=True)  38.5 us
    pallas_call x1, Pallas kernels, ocean_step(): pl.pallas_call(functools.partial(ocean_kernel, capacity, chain), out_shap...  11.6 us
    pallas_call x1, Pallas kernels, atmosphere_step(): pl.pallas_call(functools.partial(atmosphere_kernel, tiles, capacity, tile...  9.24 us
    all_to_all x1, starting transfers between devices, exchange(): lax.all_to_all(x, ('lat', 'lon'), split_axis=0, concat_axis=0, tiled=True)  6.05 us
    pallas_call x1, Pallas kernels, conv_outer(): pl.pallas_call(functools.partial(outer_kernel, count=count), out_shape=[p...  5.29 us
    pallas_call x1, Pallas kernels, conv_inner(): pl.pallas_call(inner_kernel, out_shape=[pltpu.VMEM((halves, rows, cols, L...  4.37 us
    ppermute x1, starting transfers between devices, per_device(): top = lax.ppermute(down, 'lat', north)  4.18 us
    ppermute x1, starting transfers between devices, per_device(): right = lax.ppermute(first, 'lon', [(j, i) for i, j in around])  2.95 us
  transfers between devices with their start and end apart: 5, of which 2 were waited for; matrix products, arithmetic and copies ran while one was open for 0% of the time, Pallas kernels for 13%

commit v1 on v0

--- a/solution.py
+++ b/solution.py
@@ -8,13 +8,14 @@
 from jax.sharding import PartitionSpec as P
 
 LANES = 128
-SENDS = 8
+SENDS = 2
 RIM = 8
 SIDE = 16
 VMEM_BYTES = 48 << 20
 F32, BF16 = jnp.float32, jnp.bfloat16
 ANY = pl.BlockSpec(memory_space=pl.ANY)
 IN_VMEM = pl.BlockSpec(memory_space=pltpu.VMEM)
+IN_SMEM = pl.BlockSpec(memory_space=pltpu.SMEM)
 
 
 def hbm(x):
@@ -317,7 +318,7 @@
 def atmosphere_kernel(
     tiles, capacity, tile, owner_sm, mixed_in, atm_ref, top_ref, bottom_ref, w_ref, gain_ref, up_ref, down_ref,
     flux_ref, owner_ref, mask_ref, out_ref, send_ref, rest_ref, mark_ref, mixed_ref,
-    wb, strip, fluxes, order_sm, meta, places, new_out, packets, rest, out_sems, send_sems, rest_sems,
+    wb, strip, fluxes, order_sm, count_sm, meta, places, new_out, packets, rest, out_sems, send_sems, rest_sems,
 ):
     rows, cols, channels = atm_ref.shape
     width = w_ref.shape[0]
@@ -357,7 +358,7 @@
         ],
     )
 
-    block = 16
+    block = rows
     cells = block * cols
 
     def leave(step):
@@ -403,19 +404,20 @@
     def clear(o, carry):
         for r in range(capacity):
             order_sm[o * capacity + r] = 0
-        order_sm[peers * capacity + o] = 0
+        count_sm[o] = 0
         return carry
 
-    lax.fori_loop(0, peers, clear, 0)
+    lax.fori_loop(0, peers, clear, 0, unroll=8)
 
     def count(t, carry):
         o = owner_sm[t]
-        r = order_sm[peers * capacity + o]
+        r = count_sm[o]
         order_sm[o * capacity + r] = t
-        order_sm[peers * capacity + o] = r + 1
+        count_sm[o] = r + 1
         return carry
 
-    lax.fori_loop(0, tiles, count, 0)
+    lax.fori_loop(0, tiles, count, 0, unroll=8)
+
     order = iota((packed + rest_ref.shape[1], LANES), 0)
     top_row = iota((packed, channels), 0) == 0
     group = peers // SENDS
@@ -462,7 +464,6 @@
     hidden = w_up.shape[1]
     cells = rows * cols
     remaining = -(-(capacity * tile + 1 - packed) // 16) * 16
-    in_smem = pl.BlockSpec(memory_space=pltpu.SMEM)
     return pl.pallas_call(
         functools.partial(atmosphere_kernel, tiles, capacity, tile),
         out_shape=[
@@ -472,14 +473,15 @@
             jax.ShapeDtypeStruct((8, LANES), F32),
             pltpu.VMEM(mixed.shape, F32),
         ],
-        in_specs=[in_smem] + [IN_VMEM] * 11,
+        in_specs=[IN_SMEM] + [IN_VMEM] * 11,
         out_specs=[ANY, ANY, ANY, IN_VMEM, IN_VMEM],
         input_output_aliases={1: 4},
         scratch_shapes=[
             pltpu.VMEM((halves, width * width, 8, LANES), F32),
             pltpu.VMEM((halves, margin, cols + 2 * RIM, LANES), F32),
             pltpu.VMEM((cells, channels), BF16),
-            pltpu.SMEM((peers * (capacity + 1),), jnp.int32),
+            pltpu.SMEM((peers * capacity,), jnp.int32),
+            pltpu.SMEM((peers,), jnp.int32),
             pltpu.VMEM((peers, 2 * LANES), F32),
             pltpu.VMEM((peers, LANES), jnp.int32),
             pltpu.VMEM((rows, cols, channels), BF16),
@@ -533,15 +535,18 @@
     tile = pair // capacity
     chains = peers // chain
 
+    pieces = in_sems.shape[0] // chains
+    piece = chain // pieces
+
     def arrive(i):
-        part = pl.ds(i * chain, chain)
+        part = pl.ds(i * piece, piece)
         return pltpu.make_async_copy(packet_hbm.at[part], packet_ref.at[part], in_sems.at[i])
 
     def leave(i):
-        part = pl.ds(i * chain, chain)
+        part = pl.ds(i * piece, piece)
         return pltpu.make_async_copy(out_ref.at[part], out_hbm.at[part], out_sems.at[i])
 
-    for i in range(chains):
+    for i in range(chains * pieces):
         arrive(i).start()
     ahead = jnp.where(
         iota((pair, LANES), 1) < iota((pair, LANES), 0),
@@ -551,7 +556,8 @@
     order = iota((pair, packed), 1)
 
     def mix(i, over):
-        arrive(i).wait()
+        for j in range(pieces):
+            arrive(i * pieces + j).wait()
         first = i * chain
         head = jnp.concatenate([packet_ref[first + g, 0:1, :] for g in range(chain)], axis=0)
         place = lax.dot_general(
@@ -571,12 +577,13 @@
                 at = g * pair + r * tile
                 part = jnp.where(used, result[at : at + tile], 0.0)
                 out_ref[first + g, r * tile : (r + 1) * tile, :] = part.astype(BF16)
-        leave(i).start()
+            if (g + 1) % piece == 0:
+                leave(i * pieces + g // piece).start()
         return jnp.maximum(over, jnp.max(flags[:, capacity : capacity + 1], axis=0, keepdims=True))
 
     over = lax.fori_loop(0, chains, mix, jnp.zeros((1, 1), F32))
     over_ref[0, 0] = jnp.max(over)
-    for i in range(chains):
+    for i in range(chains * pieces):
         leave(i).wait()
 
 
@@ -584,8 +591,7 @@
     peers, pair, channels = state.shape
     packed = packets.shape[1]
     hidden = w_up.shape[1]
-    chain = min(peers, 1024 // pair)
-    chains = peers // chain
+    chain = min(peers, 4096 // pair)
     cells = peers * pair
     return pl.pallas_call(
         functools.partial(ocean_kernel, capacity, chain),
@@ -594,12 +600,12 @@
             jax.ShapeDtypeStruct((1, 1), F32),
         ],
         in_specs=[IN_VMEM, ANY, IN_VMEM, IN_VMEM, IN_VMEM],
-        out_specs=[ANY, pl.BlockSpec(memory_space=pltpu.SMEM)],
+        out_specs=[ANY, IN_SMEM],
         scratch_shapes=[
             pltpu.VMEM((peers, packed, channels), BF16),
             pltpu.VMEM((peers, pair, channels), BF16),
-            pltpu.SemaphoreType.DMA((chains,)),
-            pltpu.SemaphoreType.DMA((chains,)),
+            pltpu.SemaphoreType.DMA((8,)),
+            pltpu.SemaphoreType.DMA((8,)),
         ],
         compiler_params=pltpu.CompilerParams(vmem_limit_bytes=VMEM_BYTES),
         cost_estimate=pl.CostEstimate(

time: 89 us -> 87.1 us (0.979)
  Pallas kernels: 33.7 us -> 31.5 us
    pallas_call x1, Pallas kernels: 9.24 us -> 7.52 us  [atmosphere_step(): pl.pallas_call(functools.partial(atmosphere_kernel, tiles, capacity, tile...]
where the time goes in v1:
time: 87.1 us; the launch traced here: 86.8 us
  waiting for transfers between devices  38.6 us (44%)
  Pallas kernels  31.5 us (36%)
  starting transfers between devices  15.1 us (17%)
  between operations  1.56 us (2%)
    all_to_all x1, waiting for transfers between devices, exchange(): lax.all_to_all(x, ('lat', 'lon'), split_axis=0, concat_axis=0, tiled=True)  38.4 us
    pallas_call x1, Pallas kernels, ocean_step(): pl.pallas_call(functools.partial(ocean_kernel, capacity, chain), out_shap...  11.2 us
    pallas_call x1, Pallas kernels, atmosphere_step(): pl.pallas_call(functools.partial(atmosphere_kernel, tiles, capacity, tile...  7.52 us
    all_to_all x1, starting transfers between devices, exchange(): lax.all_to_all(x, ('lat', 'lon'), split_axis=0, concat_axis=0, tiled=True)  6.23 us
    pallas_call x1, Pallas kernels, conv_outer(): pl.pallas_call(functools.partial(outer_kernel, count=count), out_shape=[p...  5.29 us
    pallas_call x1, Pallas kernels, conv_inner(): pl.pallas_call(inner_kernel, out_shape=[pltpu.VMEM((halves, rows, cols, L...  4.37 us
    ppermute x1, starting transfers between devices, per_device(): top = lax.ppermute(down, 'lat', north)  4.18 us
    ppermute x1, starting transfers between devices, per_device(): right = lax.ppermute(first, 'lon', [(j, i) for i, j in around])  2.95 us
  transfers between devices with their start and end apart: 5, of which 2 were waited for; matrix products, arithmetic and copies ran while one was open for 0% of the time, Pallas kernels for 13%

profile of v1, /device:TPU:0, one launch (start us, length us, event | category | flops | bytes accessed | tf_op | source)
XLA Modules:
  0.0 86.8 jit_solution(4597697249209664198)
XLA Ops:
  0.6 1.3 %edges.1 = (bf16[32,64,256]{2,1,0:T(8,128)(2,1)S(1)}, f32[7,7,256]{2,1,0:T(8,128)S(1)}, bf16[32,8,256]{2,1,0:T(8,128)(2,1)S(1)}, bf16[32,8,256]{2,1,0:T(8,128)(2,1)S(1)}) custom-call(bf16[32,64,256]{2,1,0:T(8,128)(2,1)} %x_ref.1, f32[7,7,256]{2,1,0:T(8,128)} %w_ref.1), custom_call_target="tpu_custom_call" | custom-call | tf_op jit(solution)/shard_map/edges/pallas_call | solution.py:134
  1.9 0.5 collective-permute-start
  2.4 2.9 %collective-permute-start.1 = (bf16[32,8,256]{2,1,0:T(8,128)(2,1)S(1)}, bf16[32,8,256]{2,1,0:T(8,128)(2,1)S(1)}, u32[]{:S(2)}, u32[]{:S(2)}) collective-permute-start(bf16[32,8,256]{2,1,0:T(8,128)(2,1)S(1)} %get-tuple-element.57), channel_id=1, source_target_pairs={{4,0},{8,4},{12,8},{16,12},{20,16},{24,20},{28,24},{0,28},{5,1},{9... | collective-permute-start | bytes 393224 | tf_op jit(solution)/shard_map/ppermute | solution.py:644
  5.4 4.4 %conv_inner.1 = (f32[2,32,64,128]{3,2,1,0:T(8,128)S(1)}, f32[2,119,8,128]{3,2,1,0:T(8,128)S(1)}) custom-call(bf16[32,64,256]{2,1,0:T(8,128)(2,1)S(1)} %get-tuple-element.53.own_ref.atm_ref, f32[7,7,256]{2,1,0:T(8,128)S(1)} %get-tuple-element.54.w_ref), custom_call_target="tpu_custom_call" | custom-call | flops 51380224 | bytes 3145728 | tf_op jit(solution)/shard_map/conv_inner/pallas_call | solution.py:190
  9.7 0.0 collective-permute-done.left_ref
  9.7 0.0 collective-permute-done.1.right_ref
  9.8 4.2 %collective-permute-start.2 = (bf16[3,80,256]{2,1,0:T(8,128)(2,1)S(1)}, bf16[3,80,256]{2,1,0:T(8,128)(2,1)S(1)}, u32[]{:S(2)}, u32[]{:S(2)}) collective-permute-start(bf16[3,80,256]{2,1,0:T(8,128)(2,1)S(1)} %get-tuple-element.60), channel_id=1, source_target_pairs={{0,1},{1,2},{2,3},{4,5},{5,6},{6,7},{8,9},{9,10},{10,11},{12,13},{... | collective-permute-start | bytes 368648 | tf_op jit(solution)/shard_map/ppermute | solution.py:648
  14.0 1.3 %collective-permute-start.3 = (bf16[3,80,256]{2,1,0:T(8,128)(2,1)S(1)}, bf16[3,80,256]{2,1,0:T(8,128)(2,1)S(1)}, u32[]{:S(2)}, u32[]{:S(2)}) collective-permute-start(bf16[3,80,256]{2,1,0:T(8,128)(2,1)S(1)} %get-tuple-element.61), channel_id=1, source_target_pairs={{1,0},{2,1},{3,2},{5,4},{6,5},{7,6},{9,8},{10,9},{11,10},{13,12},{... | collective-permute-start | bytes 368648 | tf_op jit(solution)/shard_map/ppermute | solution.py:649
  15.3 0.0 copy-start
  15.3 0.0 copy-start.1
  15.3 0.0 copy-start.2
  15.3 5.3 %conv_outer.1 = (f32[2,32,64,128]{3,2,1,0:T(8,128)S(1)}, bf16[256,1024]{1,0:T(8,128)(2,1)S(1)}, bf16[1024,256]{1,0:T(8,128)(2,1)S(1)}, bf16[256,256]{1,0:T(8,128)(2,1)S(1)}) custom-call(f32[2,32,64,128]{3,2,1,0:T(8,128)S(1)} %get-tuple-element.55.mixed_in.mixed_ref, ...), custom_call_target="tpu_custom_call", output_to_operand_aliasing={{0}: (0, {})} | custom-call | flops 12845056 | bytes 786432 | tf_op jit(solution)/shard_map/conv_outer/pallas_call | solution.py:259
  20.6 0.0 collective-permute-done.2.top_ref
  20.6 0.1 collective-permute-done.3.bottom_ref
  20.7 0.0 copy-done
  20.7 0.0 copy-done.1
  20.7 0.0 copy-done.2
  20.7 7.5 %atmosphere.1 = (bf16[32,64,256]{2,1,0:T(8,128)(2,1)}, bf16[32,104,256]{2,1,0:T(8,128)(2,1)}, bf16[32,32,256]{2,1,0:T(8,128)(2,1)}, f32[8,128]{1,0:T(8,128)S(1)}, f32[2,32,64,128]{3,2,1,0:T(8,128)S(1)}) custom-call(s32[32]{0:T(128)S(1)} %bitcast.8, f32[2,32,64,128]{3,2,1,0:T(8,128)S(1)} %get-tuple-element.59.mixed_in, ...), custom_call_target="tpu_custom_call", output_to_operand_aliasing={{4}: (1, {})} | custom-call | flops 2415919104 | bytes 6291456 | tf_op jit(solution)/shard_map/atmosphere/pallas_call | solution.py:467
  28.3 6.2 %all-to-all-start.1 = ((bf16[32,104,256]{2,1,0:T(8,128)(2,1)}), bf16[32,104,256]{2,1,0:T(8,128)(2,1)}, u32[]{:S(2)}, u32[]{:S(2)}) async-start(bf16[32,104,256]{2,1,0:T(8,128)(2,1)} %get-tuple-element.68), calls=%async_computation.1 | async-start | bytes 3407872 | tf_op jit(solution)/shard_map/all_to_all | solution.py:659
  34.5 1.9 %fetch.1 = (bf16[32,128,256]{2,1,0:T(8,128)(2,1)S(1)}, f32[1,256]{1,0:T(1,128)S(1)}, bf16[256,1024]{1,0:T(8,128)(2,1)S(1)}, bf16[1024,256]{1,0:T(8,128)(2,1)S(1)}) custom-call(f32[8,128]{1,0:T(8,128)S(1)} %get-tuple-element.66.mark_ref, bf16[32,128,256]{2,1,0:T(8,128)(2,1)} %bitcast.10, f32[1,256]{1,0:T(1,128)} %bitcast.11, bf16[256,1024]{1,0:T(8,128)(2,1)} %refs_2_.3, ...), custom_call_target="tpu_custom_call" | custom-call | tf_op jit(solution)/shard_map/fetch/pallas_call | solution.py:518
  36.4 38.4 %all-to-all-done.1.packet_hbm = bf16[32,104,256]{2,1,0:T(8,128)(2,1)} async-done(((bf16[32,104,256]{2,1,0:T(8,128)(2,1)}), bf16[32,104,256]{2,1,0:T(8,128)(2,1)}, u32[]{:S(2)}, u32[]{:S(2)}) %all-to-all-start.1) | async-done | bytes 1703968 | tf_op jit(solution)/shard_map/all_to_all | solution.py:659
  74.8 0.0 copy-start.3
  74.8 11.2 %ocean.3 = (bf16[32,128,256]{2,1,0:T(8,128)(2,1)}, f32[1,1]{1,0:T(1,128)}) custom-call(bf16[32,128,256]{2,1,0:T(8,128)(2,1)S(1)} %get-tuple-element.67.state_ref, bf16[32,104,256]{2,1,0:T(8,128)(2,1)} %all-to-all-done.1.packet_hbm, f32[1,256]{1,0:T(1,128)S(1)} %get-tuple-element.69.gain_ref, bf16[256,1024]{1,0:T(8,128)(2,1)S(1)} %get-tuple-element.70.up_ref, ...), custom_call_target="tpu_custom_call" | custom-call | flops 4294967296 | bytes 6291456 | tf_op jit(solution)/shard_map/ocean/pallas_call | solution.py:596
  86.6 0.0 copy-done.3
  (2 shorter events, 0.0 us)
Async XLA Ops:
  1.9 7.8 %collective-permute-start = (bf16[32,8,256]{2,1,0:T(8,128)(2,1)S(1)}, bf16[32,8,256]{2,1,0:T(8,128)(2,1)S(1)}, u32[]{:S(2)}, u32[]{:S(2)}) collective-permute-start(bf16[32,8,256]{2,1,0:T(8,128)(2,1)S(1)} %get-tuple-element.56), channel_id=1, source_target_pairs={{0,4},{4,8},{8,12},{12,16},{16,20},{20,24},{24,28},{28,0},{1,5},{5... | collective-permute-start | bytes 393224 | tf_op jit(solution)/shard_map/ppermute | solution.py:643
  2.4 7.3 %collective-permute-start.1 = (bf16[32,8,256]{2,1,0:T(8,128)(2,1)S(1)}, bf16[32,8,256]{2,1,0:T(8,128)(2,1)S(1)}, u32[]{:S(2)}, u32[]{:S(2)}) collective-permute-start(bf16[32,8,256]{2,1,0:T(8,128)(2,1)S(1)} %get-tuple-element.57), channel_id=1, source_target_pairs={{4,0},{8,4},{12,8},{16,12},{20,16},{24,20},{28,24},{0,28},{5,1},{9... | collective-permute-start | bytes 393224 | tf_op jit(solution)/shard_map/ppermute | solution.py:644
  9.8 10.8 %collective-permute-start.2 = (bf16[3,80,256]{2,1,0:T(8,128)(2,1)S(1)}, bf16[3,80,256]{2,1,0:T(8,128)(2,1)S(1)}, u32[]{:S(2)}, u32[]{:S(2)}) collective-permute-start(bf16[3,80,256]{2,1,0:T(8,128)(2,1)S(1)} %get-tuple-element.60), channel_id=1, source_target_pairs={{0,1},{1,2},{2,3},{4,5},{5,6},{6,7},{8,9},{9,10},{10,11},{12,13},{... | collective-permute-start | bytes 368648 | tf_op jit(solution)/shard_map/ppermute | solution.py:648
  14.0 6.8 %collective-permute-start.3 = (bf16[3,80,256]{2,1,0:T(8,128)(2,1)S(1)}, bf16[3,80,256]{2,1,0:T(8,128)(2,1)S(1)}, u32[]{:S(2)}, u32[]{:S(2)}) collective-permute-start(bf16[3,80,256]{2,1,0:T(8,128)(2,1)S(1)} %get-tuple-element.61), channel_id=1, source_target_pairs={{1,0},{2,1},{3,2},{5,4},{6,5},{7,6},{9,8},{10,9},{11,10},{13,12},{... | collective-permute-start | bytes 368648 | tf_op jit(solution)/shard_map/ppermute | solution.py:649
  15.3 5.5 %copy-start = (s32[32,64]{1,0:T(8,128)S(1)}, s32[32,64]{1,0:T(8,128)}, u32[]{:S(2)}) copy-start(s32[32,64]{1,0:T(8,128)} %mask_ref.1) | copy-start | bytes 24580
  15.3 5.5 %copy-start.1 = (f32[256]{0:T(256)S(1)}, f32[256]{0:T(256)}, u32[]{:S(2)}) copy-start(f32[256]{0:T(256)} %param.16) | copy-start | bytes 3076
  15.3 5.5 %copy-start.2 = (s32[1,1,32]{2,1,0:T(1,128)S(1)}, s32[1,1,32]{2,1,0:T(1,128)}, u32[]{:S(2)}) copy-start(s32[1,1,32]{2,1,0:T(1,128)} %param.21) | copy-start | bytes 388
  28.3 46.6 %all-to-all-start.1 = ((bf16[32,104,256]{2,1,0:T(8,128)(2,1)}), bf16[32,104,256]{2,1,0:T(8,128)(2,1)}, u32[]{:S(2)}, u32[]{:S(2)}) async-start(bf16[32,104,256]{2,1,0:T(8,128)(2,1)} %get-tuple-element.68), calls=%async_computation.1 | async-start | bytes 3407872 | tf_op jit(solution)/shard_map/all_to_all | solution.py:659
  74.8 11.8 %copy-start.3 = (bf16[32,32,256]{2,1,0:T(8,128)(2,1)S(1)}, bf16[32,32,256]{2,1,0:T(8,128)(2,1)}, u32[]{:S(2)}) copy-start(bf16[32,32,256]{2,1,0:T(8,128)(2,1)} %get-tuple-element.74) | copy-start | bytes 1572868

commit v2 on v1

--- a/solution.py
+++ b/solution.py
@@ -150,38 +150,36 @@
 GROUP = 8
 
 
-def inner_kernel(own_ref, w_ref, mixed_ref, wb, fs):
+def inner_kernel(own_ref, w_ref, mixed_ref, wb, xs, fs):
     rows, cols, channels = own_ref.shape
     spread_products(w_ref, wb)
     halves = channels // LANES
     first = SIDE - RIM
+    each = (cols - 2 * SIDE) // 8
     for h in range(halves):
-        part = slice(h * LANES, (h + 1) * LANES)
-
-        def prepare(c, carry):
-            c0 = pl.multiple_of(c * 16, 16)
+        xs[h] = own_ref[:, first : cols - first, h * LANES : (h + 1) * LANES].astype(F32)
+
+    def prepare(t, carry):
+        for h in range(halves):
 
             def put(k, m, value):
-                fs[h, k, m, pl.ds(c0, 16)] = value
-
-            combine_rows(lambda r: own_ref[r, pl.ds(c0 + first, 16), part].astype(F32), put, rows)
-            return carry
-
-        lax.fori_loop(0, fs.shape[3] // 16, prepare, 0)
-    blocks = (cols - 2 * SIDE) // 8
+                fs[h, k, m, t] = value
+
+            combine_rows(lambda r: xs[h, r, pl.ds(RIM - MARGIN + t, 8, stride=each)], put, rows)
+        return carry
+
+    lax.fori_loop(0, each + 2 * MARGIN, prepare, 0)
 
     def body(step, carry):
-        m0 = (step // blocks) * GROUP
-        c0 = pl.multiple_of((step % blocks) * 8, 8)
+        m0 = (step // each) * GROUP
+        t = step % each
         for h in range(halves):
-            out = filter_rows(
-                lambda k, m, q: fs[h, k, m0 + m, pl.ds(c0 + (RIM - MARGIN + q), 8)], wb, h, GROUP
-            )
+            out = filter_rows(lambda k, m, q: fs[h, k, m0 + m, t + q], wb, h, GROUP)
             for i, value in enumerate(out):
-                mixed_ref[h, m0 * 4 + i, pl.ds(c0 + SIDE, 8)] = value
+                mixed_ref[h, m0 * 4 + i, pl.ds(SIDE + t, 8, stride=each)] = value
         return carry
 
-    lax.fori_loop(0, (rows // 4 // GROUP) * blocks, body, 0)
+    lax.fori_loop(0, (rows // 4 // GROUP) * each, body, 0)
 
 
 def conv_inner(own, conv_weight):
@@ -196,7 +194,8 @@
         in_specs=[IN_VMEM, IN_VMEM],
         out_specs=[IN_VMEM, IN_VMEM],
         scratch_shapes=[
-            pltpu.VMEM((halves, len(PRODUCTS), rows // 4 + 1, cols - 2 * (SIDE - RIM), LANES), F32),
+            pltpu.VMEM((halves, rows, cols - 2 * (SIDE - RIM), LANES), F32),
+            pltpu.VMEM((halves, len(PRODUCTS), rows // 4 + 1, (cols - 2 * SIDE) // 8 + 2 * MARGIN, 8, LANES), F32),
         ],
         compiler_params=pltpu.CompilerParams(vmem_limit_bytes=VMEM_BYTES),
         cost_estimate=pl.CostEstimate(
@@ -274,13 +273,19 @@
     )(vmem(mixed), vmem(own), vmem(left), vmem(right), vmem(products), *[hbm(w) for w in weights])
 
 
-def widen_kernel(own_ref, left_ref, right_ref, mixed_ref, up_ref, down_ref):
-    margin = up_ref.shape[0]
+def even_latitude():
+    return lax.rem(lax.axis_index("lat"), 2) == 0
+
+
+def widen_kernel(own_ref, left_ref, right_ref, mixed_ref, even_ref, odd_ref):
+    margin = even_ref.shape[0]
     rows, cols, _ = own_ref.shape
-    for out, at in ((up_ref, 0), (down_ref, rows - margin)):
-        out[:, 0:RIM] = left_ref[at : at + margin]
-        out[:, RIM : RIM + cols] = own_ref[at : at + margin]
-        out[:, RIM + cols :] = right_ref[at : at + margin]
+    last = jnp.where(even_latitude(), rows - margin, 0)
+    for out, at in ((even_ref, last), (odd_ref, rows - margin - last)):
+        part = pl.ds(at, margin)
+        out[:, 0:RIM] = left_ref[part]
+        out[:, RIM : RIM + cols] = own_ref[part]
+        out[:, RIM + cols :] = right_ref[part]
 
 
 def widen(own, left, right, mixed, margin):
@@ -316,7 +321,7 @@
 
 
 def atmosphere_kernel(
-    tiles, capacity, tile, owner_sm, mixed_in, atm_ref, top_ref, bottom_ref, w_ref, gain_ref, up_ref, down_ref,
+    tiles, capacity, tile, owner_sm, mixed_in, atm_ref, even_ref, odd_ref, w_ref, gain_ref, up_ref, down_ref,
     flux_ref, owner_ref, mask_ref, out_ref, send_ref, rest_ref, mark_ref, mixed_ref,
     wb, strip, fluxes, order_sm, count_sm, meta, places, new_out, packets, rest, out_sems, send_sems, rest_sems,
 ):
@@ -332,9 +337,12 @@
 
     spread_weights(w_ref, wb, width)
 
-    def latitude(rows_ref, pairs):
+    even = even_latitude()
+
+    def latitude(if_even, if_odd, pairs):
         for h in range(halves):
-            strip[h] = rows_ref[:, :, lanes(h)].astype(F32)
+            rows_in = [ref[:, :, lanes(h)].astype(F32) for ref in (if_even, if_odd)]
+            strip[h] = jnp.where(even, *rows_in)
 
         def body(c, carry):
             c0 = pl.multiple_of(c * 8, 8)
@@ -349,9 +357,10 @@
 
         lax.fori_loop(0, cols // 8, body, 0)
 
-    latitude(top_ref, [(i, [(i + p, p) for p in range(margin - i)]) for i in range(margin)])
+    latitude(odd_ref, even_ref, [(i, [(i + p, p) for p in range(margin - i)]) for i in range(margin)])
     latitude(
-        bottom_ref,
+        even_ref,
+        odd_ref,
         [
             (rows - margin + i, [(i - e, width - 1 - e) for e in range(i + 1)])
             for i in range(margin)
@@ -454,7 +463,7 @@
 
 
 def atmosphere_step(
-    mixed, own, top, bottom, conv_weight, gain, w_up, w_down, w_flux, owners, mask, peers, capacity, tile, packed
+    mixed, own, from_even, from_odd, conv_weight, gain, w_up, w_down, w_flux, owners, mask, peers, capacity, tile, packed
 ):
     rows, cols, channels = own.shape
     tiles = owners.shape[0]
@@ -498,7 +507,7 @@
         ),
         name="atmosphere",
     )(
-        owners, vmem(mixed), vmem(own), vmem(top), vmem(bottom), vmem(conv_weight), gain.reshape(1, -1), vmem(w_up),
+        owners, vmem(mixed), vmem(own), vmem(from_even), vmem(from_odd), vmem(conv_weight), gain.reshape(1, -1), vmem(w_up),
         vmem(w_down), vmem(w_flux), owners.reshape(1, -1), mask,
     )
 
@@ -553,7 +562,7 @@
         1.0,
         jnp.where(iota((pair, LANES), 1) == iota((pair, LANES), 0), 1000.0, 0.0),
     ).astype(BF16)
-    order = iota((pair, packed), 1)
+    order = iota((pair, packed), 1).astype(F32).astype(BF16)
 
     def mix(i, over):
         for j in range(pieces):
@@ -563,11 +572,11 @@
         place = lax.dot_general(
             ahead, head[:, 0:LANES], (((1,), (1,)), ((), ())), preferred_element_type=F32
         )
-        place = (place - 999.0).astype(jnp.int32)
+        place = (place - 999.0).astype(BF16)
         flags = head[:, LANES:].astype(F32)
         states = []
         for g in range(chain):
-            pick = jnp.where(order == place[:, g : g + 1], 1.0, 0.0).astype(BF16)
+            pick = jnp.where(order == place[:, g : g + 1], jnp.ones_like(order), jnp.zeros_like(order))
             states.append(state_ref[first + g].astype(F32) + dot(pick, packet_ref[first + g]))
         states = jnp.concatenate(states, axis=0)
         result = states + mixer(normalize(states, gain_ref[...]), up_ref, down_ref)
@@ -643,15 +652,18 @@
     left = lax.ppermute(last, "lon", around)
     right = lax.ppermute(first, "lon", [(j, i) for i, j in around])
     mixed, products = conv_inner(own, conv_weight)
-    up, down = widen(own, left, right, mixed, margin)
-    north = [(i, i + 1) for i in range(n_lat - 1)]
-    top = lax.ppermute(down, "lat", north)
-    bottom = lax.ppermute(up, "lat", [(j, i) for i, j in north])
+    to_even, to_odd = widen(own, left, right, mixed, margin)
+
+    def swap(x, first):
+        pairs = [(i, i + 1) for i in range(first, n_lat - 1, 2)]
+        return lax.ppermute(x, "lat", pairs + [(j, i) for i, j in pairs])
+
+    from_even, from_odd = swap(to_even, 0), swap(to_odd, 1)
     mixed, w_up, w_down, w_flux = conv_outer(
         mixed, own, left, right, products, (atm_up, atm_down, flux_weight)
     )
     atm_out, packets, rest, mark, _ = atmosphere_step(
-        mixed, own, top, bottom, conv_weight, atm_gain, w_up, w_down, w_flux, owners,
+        mixed, own, from_even, from_odd, conv_weight, atm_gain, w_up, w_down, w_flux, owners,
         land_mask.reshape(owners.shape[0], tile), peers, capacity, tile, packed,
     )
 

time: 87.1 us -> 84.2 us (0.967)
  starting transfers between devices: 15.1 us -> 12.5 us
    ppermute x2, starting transfers between devices: 5.47 us -> 2.99 us  [swap(): return lax.ppermute(x, 'lat', pairs + [(j, i) for i, j in pairs])]
  transfers between devices with their start and end apart: 5 -> 5, of which waited for: 2 -> 1; matrix products, arithmetic and copies ran while one was open for 0% -> 0% of each run, Pallas kernels for 13% -> 14%
where the time goes in v2:
time: 84.2 us; the launch traced here: 83.9 us
  waiting for transfers between devices  38.4 us (46%)
  Pallas kernels  31.4 us (37%)
  starting transfers between devices  12.5 us (15%)
  between operations  1.59 us (2%)
    all_to_all x1, waiting for transfers between devices, exchange(): lax.all_to_all(x, ('lat', 'lon'), split_axis=0, concat_axis=0, tiled=True)  38.4 us
    pallas_call x1, Pallas kernels, ocean_step(): pl.pallas_call(functools.partial(ocean_kernel, capacity, chain), out_shap...  10.9 us
    pallas_call x1, Pallas kernels, atmosphere_step(): pl.pallas_call(functools.partial(atmosphere_kernel, tiles, capacity, tile...  7.56 us
    all_to_all x1, starting transfers between devices, exchange(): lax.all_to_all(x, ('lat', 'lon'), split_axis=0, concat_axis=0, tiled=True)  6.05 us
    pallas_call x1, Pallas kernels, conv_outer(): pl.pallas_call(functools.partial(outer_kernel, count=count), out_shape=[p...  5.29 us
    pallas_call x1, Pallas kernels, conv_inner(): pl.pallas_call(inner_kernel, out_shape=[pltpu.VMEM((halves, rows, cols, L...  4.4 us
    ppermute x2, starting transfers between devices, swap(): return lax.ppermute(x, 'lat', pairs + [(j, i) for i, j in pairs])  2.99 us
    ppermute x1, starting transfers between devices, per_device(): right = lax.ppermute(first, 'lon', [(j, i) for i, j in around])  2.95 us
  transfers between devices with their start and end apart: 5, of which 1 were waited for; matrix products, arithmetic and copies ran while one was open for 0% of the time, Pallas kernels for 14%

profile of v2, /device:TPU:0, one launch (start us, length us, event | category | flops | bytes accessed | tf_op | source)
XLA Modules:
  0.0 83.9 jit_solution(15517587310587775106)
XLA Ops:
  0.6 1.3 %edges.1 = (bf16[32,64,256]{2,1,0:T(8,128)(2,1)S(1)}, f32[7,7,256]{2,1,0:T(8,128)S(1)}, bf16[32,8,256]{2,1,0:T(8,128)(2,1)S(1)}, bf16[32,8,256]{2,1,0:T(8,128)(2,1)S(1)}) custom-call(bf16[32,64,256]{2,1,0:T(8,128)(2,1)} %x_ref.1, f32[7,7,256]{2,1,0:T(8,128)} %w_ref.1), custom_call_target="tpu_custom_call" | custom-call | tf_op jit(solution)/shard_map/edges/pallas_call | solution.py:134
  1.9 0.5 collective-permute-start
  2.4 2.9 %collective-permute-start.1 = (bf16[32,8,256]{2,1,0:T(8,128)(2,1)S(1)}, bf16[32,8,256]{2,1,0:T(8,128)(2,1)S(1)}, u32[]{:S(2)}, u32[]{:S(2)}) collective-permute-start(bf16[32,8,256]{2,1,0:T(8,128)(2,1)S(1)} %get-tuple-element.57), channel_id=1, source_target_pairs={{4,0},{8,4},{12,8},{16,12},{20,16},{24,20},{28,24},{0,28},{5,1},{9... | collective-permute-start | bytes 393224 | tf_op jit(solution)/shard_map/ppermute | solution.py:653
  5.4 4.4 %conv_inner.1 = (f32[2,32,64,128]{3,2,1,0:T(8,128)S(1)}, f32[2,119,8,128]{3,2,1,0:T(8,128)S(1)}) custom-call(bf16[32,64,256]{2,1,0:T(8,128)(2,1)S(1)} %get-tuple-element.53.own_ref.atm_ref, f32[7,7,256]{2,1,0:T(8,128)S(1)} %get-tuple-element.54.w_ref), custom_call_target="tpu_custom_call" | custom-call | flops 51380224 | bytes 3145728 | tf_op jit(solution)/shard_map/conv_inner/pallas_call | solution.py:188
  9.8 0.0 collective-permute-done.left_ref
  9.8 0.0 collective-permute-done.1.right_ref
  9.8 2.3 %collective-permute-start.2 = (bf16[3,80,256]{2,1,0:T(8,128)(2,1)S(1)}, bf16[3,80,256]{2,1,0:T(8,128)(2,1)S(1)}, u32[]{:S(2)}, u32[]{:S(2)}) collective-permute-start(bf16[3,80,256]{2,1,0:T(8,128)(2,1)S(1)} %get-tuple-element.60), channel_id=1, source_target_pairs={{0,1},{2,3},{1,0},{3,2},{4,5},{6,7},{5,4},{7,6},{8,9},{10,11},{9,8... | collective-permute-start | bytes 368648 | tf_op jit(solution)/shard_map/ppermute | solution.py:659
  12.2 0.7 collective-permute-start.3
  12.8 0.0 copy-start
  12.8 0.0 copy-start.1
  12.8 0.0 copy-start.2
  12.9 5.3 %conv_outer.1 = (f32[2,32,64,128]{3,2,1,0:T(8,128)S(1)}, bf16[256,1024]{1,0:T(8,128)(2,1)S(1)}, bf16[1024,256]{1,0:T(8,128)(2,1)S(1)}, bf16[256,256]{1,0:T(8,128)(2,1)S(1)}) custom-call(f32[2,32,64,128]{3,2,1,0:T(8,128)S(1)} %get-tuple-element.55.mixed_in.mixed_ref, ...), custom_call_target="tpu_custom_call", output_to_operand_aliasing={{0}: (0, {})} | custom-call | flops 12845056 | bytes 786432 | tf_op jit(solution)/shard_map/conv_outer/pallas_call | solution.py:258
  18.2 0.0 collective-permute-done.2.even_ref
  18.2 0.0 collective-permute-done.3.odd_ref
  18.2 0.0 copy-done
  18.2 0.0 copy-done.1
  18.2 0.0 copy-done.2
  18.2 7.6 %atmosphere.1 = (bf16[32,64,256]{2,1,0:T(8,128)(2,1)}, bf16[32,104,256]{2,1,0:T(8,128)(2,1)}, bf16[32,32,256]{2,1,0:T(8,128)(2,1)}, f32[8,128]{1,0:T(8,128)S(1)}, f32[2,32,64,128]{3,2,1,0:T(8,128)S(1)}) custom-call(s32[32]{0:T(128)S(1)} %bitcast.8, f32[2,32,64,128]{3,2,1,0:T(8,128)S(1)} %get-tuple-element.59.mixed_in, ...), custom_call_target="tpu_custom_call", output_to_operand_aliasing={{4}: (1, {})} | custom-call | flops 2415919104 | bytes 6291456 | tf_op jit(solution)/shard_map/atmosphere/pallas_call | solution.py:476
  25.8 6.1 %all-to-all-start.1 = ((bf16[32,104,256]{2,1,0:T(8,128)(2,1)}), bf16[32,104,256]{2,1,0:T(8,128)(2,1)}, u32[]{:S(2)}, u32[]{:S(2)}) async-start(bf16[32,104,256]{2,1,0:T(8,128)(2,1)} %get-tuple-element.68), calls=%async_computation.1 | async-start | bytes 3407872 | tf_op jit(solution)/shard_map/all_to_all | solution.py:671
  31.8 1.9 %fetch.1 = (bf16[32,128,256]{2,1,0:T(8,128)(2,1)S(1)}, f32[1,256]{1,0:T(1,128)S(1)}, bf16[256,1024]{1,0:T(8,128)(2,1)S(1)}, bf16[1024,256]{1,0:T(8,128)(2,1)S(1)}) custom-call(f32[8,128]{1,0:T(8,128)S(1)} %get-tuple-element.66.mark_ref, bf16[32,128,256]{2,1,0:T(8,128)(2,1)} %bitcast.10, f32[1,256]{1,0:T(1,128)} %bitcast.11, bf16[256,1024]{1,0:T(8,128)(2,1)} %refs_2_.3, ...), custom_call_target="tpu_custom_call" | custom-call | tf_op jit(solution)/shard_map/fetch/pallas_call | solution.py:527
  33.7 38.4 %all-to-all-done.1.packet_hbm = bf16[32,104,256]{2,1,0:T(8,128)(2,1)} async-done(((bf16[32,104,256]{2,1,0:T(8,128)(2,1)}), bf16[32,104,256]{2,1,0:T(8,128)(2,1)}, u32[]{:S(2)}, u32[]{:S(2)}) %all-to-all-start.1) | async-done | bytes 1703968 | tf_op jit(solution)/shard_map/all_to_all | solution.py:671
  72.2 0.0 copy-start.3
  72.2 10.9 %ocean.3 = (bf16[32,128,256]{2,1,0:T(8,128)(2,1)}, f32[1,1]{1,0:T(1,128)}) custom-call(bf16[32,128,256]{2,1,0:T(8,128)(2,1)S(1)} %get-tuple-element.67.state_ref, bf16[32,104,256]{2,1,0:T(8,128)(2,1)} %all-to-all-done.1.packet_hbm, f32[1,256]{1,0:T(1,128)S(1)} %get-tuple-element.69.gain_ref, bf16[256,1024]{1,0:T(8,128)(2,1)S(1)} %get-tuple-element.70.up_ref, ...), custom_call_target="tpu_custom_call" | custom-call | flops 4294967296 | bytes 6291456 | tf_op jit(solution)/shard_map/ocean/pallas_call | solution.py:605
  83.7 0.0 copy-done.3
  (2 shorter events, 0.0 us)
Async XLA Ops:
  1.9 7.9 %collective-permute-start = (bf16[32,8,256]{2,1,0:T(8,128)(2,1)S(1)}, bf16[32,8,256]{2,1,0:T(8,128)(2,1)S(1)}, u32[]{:S(2)}, u32[]{:S(2)}) collective-permute-start(bf16[32,8,256]{2,1,0:T(8,128)(2,1)S(1)} %get-tuple-element.56), channel_id=1, source_target_pairs={{0,4},{4,8},{8,12},{12,16},{16,20},{20,24},{24,28},{28,0},{1,5},{5... | collective-permute-start | bytes 393224 | tf_op jit(solution)/shard_map/ppermute | solution.py:652
  2.4 7.4 %collective-permute-start.1 = (bf16[32,8,256]{2,1,0:T(8,128)(2,1)S(1)}, bf16[32,8,256]{2,1,0:T(8,128)(2,1)S(1)}, u32[]{:S(2)}, u32[]{:S(2)}) collective-permute-start(bf16[32,8,256]{2,1,0:T(8,128)(2,1)S(1)} %get-tuple-element.57), channel_id=1, source_target_pairs={{4,0},{8,4},{12,8},{16,12},{20,16},{24,20},{28,24},{0,28},{5,1},{9... | collective-permute-start | bytes 393224 | tf_op jit(solution)/shard_map/ppermute | solution.py:653
  9.8 8.3 %collective-permute-start.2 = (bf16[3,80,256]{2,1,0:T(8,128)(2,1)S(1)}, bf16[3,80,256]{2,1,0:T(8,128)(2,1)S(1)}, u32[]{:S(2)}, u32[]{:S(2)}) collective-permute-start(bf16[3,80,256]{2,1,0:T(8,128)(2,1)S(1)} %get-tuple-element.60), channel_id=1, source_target_pairs={{0,1},{2,3},{1,0},{3,2},{4,5},{6,7},{5,4},{7,6},{8,9},{10,11},{9,8... | collective-permute-start | bytes 368648 | tf_op jit(solution)/shard_map/ppermute | solution.py:659
  12.2 6.0 %collective-permute-start.3 = (bf16[3,80,256]{2,1,0:T(8,128)(2,1)S(1)}, bf16[3,80,256]{2,1,0:T(8,128)(2,1)S(1)}, u32[]{:S(2)}, u32[]{:S(2)}) collective-permute-start(bf16[3,80,256]{2,1,0:T(8,128)(2,1)S(1)} %get-tuple-element.61), channel_id=1, source_target_pairs={{1,2},{2,1},{5,6},{6,5},{9,10},{10,9},{13,14},{14,13},{17,18},{18,... | collective-permute-start | bytes 368648 | tf_op jit(solution)/shard_map/ppermute | solution.py:659
  12.8 5.4 %copy-start = (s32[32,64]{1,0:T(8,128)S(1)}, s32[32,64]{1,0:T(8,128)}, u32[]{:S(2)}) copy-start(s32[32,64]{1,0:T(8,128)} %mask_ref.1) | copy-start | bytes 24580
  12.8 5.4 %copy-start.1 = (f32[256]{0:T(256)S(1)}, f32[256]{0:T(256)}, u32[]{:S(2)}) copy-start(f32[256]{0:T(256)} %param.16) | copy-start | bytes 3076
  12.8 5.4 %copy-start.2 = (s32[1,1,32]{2,1,0:T(1,128)S(1)}, s32[1,1,32]{2,1,0:T(1,128)}, u32[]{:S(2)}) copy-start(s32[1,1,32]{2,1,0:T(1,128)} %param.21) | copy-start | bytes 388
  25.8 46.4 %all-to-all-start.1 = ((bf16[32,104,256]{2,1,0:T(8,128)(2,1)}), bf16[32,104,256]{2,1,0:T(8,128)(2,1)}, u32[]{:S(2)}, u32[]{:S(2)}) async-start(bf16[32,104,256]{2,1,0:T(8,128)(2,1)} %get-tuple-element.68), calls=%async_computation.1 | async-start | bytes 3407872 | tf_op jit(solution)/shard_map/all_to_all | solution.py:671
  72.2 11.6 %copy-start.3 = (bf16[32,32,256]{2,1,0:T(8,128)(2,1)S(1)}, bf16[32,32,256]{2,1,0:T(8,128)(2,1)}, u32[]{:S(2)}) copy-start(bf16[32,32,256]{2,1,0:T(8,128)(2,1)} %get-tuple-element.74) | copy-start | bytes 1572868

commit v3 on v2

--- a/solution.py
+++ b/solution.py
@@ -115,7 +115,11 @@
     return out
 
 
-def edges_kernel(x_ref, w_ref, own_ref, kept_ref, first_ref, last_ref, sems):
+def even_band(axis):
+    return lax.rem(lax.axis_index(axis), 2) == 0
+
+
+def edges_kernel(x_ref, w_ref, own_ref, kept_ref, even_ref, odd_ref, sems):
     cols = own_ref.shape[1]
     copies = [
         pltpu.make_async_copy(x_ref, own_ref, sems.at[0]),
@@ -125,8 +129,17 @@
         copy.start()
     for copy in copies:
         copy.wait()
-    first_ref[...] = own_ref[:, 0:RIM]
-    last_ref[...] = own_ref[:, cols - RIM :]
+    even = even_band("lon")
+
+    @pl.when(even)
+    def _():
+        even_ref[...] = own_ref[:, cols - RIM :]
+        odd_ref[...] = own_ref[:, 0:RIM]
+
+    @pl.when(jnp.logical_not(even))
+    def _():
+        even_ref[...] = own_ref[:, 0:RIM]
+        odd_ref[...] = own_ref[:, cols - RIM :]
 
 
 def edges(atmosphere, conv_weight):
@@ -205,7 +218,7 @@
     )(vmem(own), vmem(conv_weight))
 
 
-def outer_kernel(mixed_in, own_ref, left_ref, right_ref, wb, *refs, count):
+def outer_kernel(mixed_in, own_ref, even_ref, odd_ref, wb, *refs, count):
     far, mixed_ref, near = refs[:count], refs[count], refs[count + 1 : 2 * count + 1]
     fs, sems = refs[2 * count + 1 :]
     fetches = [pltpu.make_async_copy(f, n, sems.at[i]) for i, (f, n) in enumerate(zip(far, near))]
@@ -214,8 +227,9 @@
     rows, cols, channels = own_ref.shape
     halves = channels // LANES
     blocks = SIDE // 8
+    even = even_band("lon")
     for side in range(2):
-        rim, edge = (left_ref, 0) if side == 0 else (right_ref, SIDE + RIM)
+        rims, edge = ((odd_ref, even_ref), 0) if side == 0 else ((even_ref, odd_ref), SIDE + RIM)
         body_at, own_at = (RIM, 0) if side == 0 else (0, cols - SIDE - RIM)
         for h in range(halves):
             part = slice(h * LANES, (h + 1) * LANES)
@@ -223,7 +237,9 @@
             def put_rim(k, m, value):
                 fs[k, m, edge : edge + RIM] = value
 
-            combine_rows(lambda r: rim[r, :, part].astype(F32), put_rim, rows)
+            combine_rows(
+                lambda r: jnp.where(even, *[rim[r, :, part].astype(F32) for rim in rims]), put_rim, rows
+            )
 
             def prepare(c, carry):
                 c0 = pl.multiple_of(c * 8, 8)
@@ -273,19 +289,23 @@
     )(vmem(mixed), vmem(own), vmem(left), vmem(right), vmem(products), *[hbm(w) for w in weights])
 
 
-def even_latitude():
-    return lax.rem(lax.axis_index("lat"), 2) == 0
-
-
-def widen_kernel(own_ref, left_ref, right_ref, mixed_ref, even_ref, odd_ref):
+def widen_kernel(own_ref, lon_even_ref, lon_odd_ref, mixed_ref, even_ref, odd_ref):
     margin = even_ref.shape[0]
     rows, cols, _ = own_ref.shape
-    last = jnp.where(even_latitude(), rows - margin, 0)
+    last = jnp.where(even_band("lat"), rows - margin, 0)
     for out, at in ((even_ref, last), (odd_ref, rows - margin - last)):
         part = pl.ds(at, margin)
-        out[:, 0:RIM] = left_ref[part]
         out[:, RIM : RIM + cols] = own_ref[part]
-        out[:, RIM + cols :] = right_ref[part]
+
+        @pl.when(even_band("lon"))
+        def _(out=out, part=part):
+            out[:, 0:RIM] = lon_odd_ref[part]
+            out[:, RIM + cols :] = lon_even_ref[part]
+
+        @pl.when(jnp.logical_not(even_band("lon")))
+        def _(out=out, part=part):
+            out[:, 0:RIM] = lon_even_ref[part]
+            out[:, RIM + cols :] = lon_odd_ref[part]
 
 
 def widen(own, left, right, mixed, margin):
@@ -337,7 +357,7 @@
 
     spread_weights(w_ref, wb, width)
 
-    even = even_latitude()
+    even = even_band("lat")
 
     def latitude(if_even, if_odd, pairs):
         for h in range(halves):
@@ -647,12 +667,15 @@
     owners = tile_owner.reshape(-1)
     state = ocean_state.reshape(peers, pair, channels)
 
-    around = [(i, (i + 1) % n_lon) for i in range(n_lon)]
-    own, conv_weight, first, last = edges(atmosphere, conv_weight)
-    left = lax.ppermute(last, "lon", around)
-    right = lax.ppermute(first, "lon", [(j, i) for i, j in around])
+    own, conv_weight, lon_even, lon_odd = edges(atmosphere, conv_weight)
+
+    def swap_around(x, first):
+        pairs = [(i, (i + 1) % n_lon) for i in range(first, n_lon, 2)]
+        return lax.ppermute(x, "lon", pairs + [(j, i) for i, j in pairs])
+
+    lon_odd, lon_even = swap_around(lon_odd, 1), swap_around(lon_even, 0)
     mixed, products = conv_inner(own, conv_weight)
-    to_even, to_odd = widen(own, left, right, mixed, margin)
+    to_even, to_odd = widen(own, lon_even, lon_odd, mixed, margin)
 
     def swap(x, first):
         pairs = [(i, i + 1) for i in range(first, n_lat - 1, 2)]
@@ -660,7 +683,7 @@
 
     from_even, from_odd = swap(to_even, 0), swap(to_odd, 1)
     mixed, w_up, w_down, w_flux = conv_outer(
-        mixed, own, left, right, products, (atm_up, atm_down, flux_weight)
+        mixed, own, lon_even, lon_odd, products, (atm_up, atm_down, flux_weight)
     )
     atm_out, packets, rest, mark, _ = atmosphere_step(
         mixed, own, from_even, from_odd, conv_weight, atm_gain, w_up, w_down, w_flux, owners,

time: 84.2 us -> 83.5 us (level)
  no operation moved by 1% of the time
where the time goes in v3:
time: 83.5 us; the launch traced here: 83.3 us
  waiting for transfers between devices  38.4 us (46%)
  Pallas kernels  31.4 us (38%)
  starting transfers between devices  11.8 us (14%)
  between operations  1.59 us (2%)
    all_to_all x1, waiting for transfers between devices, exchange(): lax.all_to_all(x, ('lat', 'lon'), split_axis=0, concat_axis=0, tiled=True)  38.4 us
    pallas_call x1, Pallas kernels, ocean_step(): pl.pallas_call(functools.partial(ocean_kernel, capacity, chain), out_shap...  10.9 us
    pallas_call x1, Pallas kernels, atmosphere_step(): pl.pallas_call(functools.partial(atmosphere_kernel, tiles, capacity, tile...  7.56 us
    all_to_all x1, starting transfers between devices, exchange(): lax.all_to_all(x, ('lat', 'lon'), split_axis=0, concat_axis=0, tiled=True)  5.43 us
    pallas_call x1, Pallas kernels, conv_outer(): pl.pallas_call(functools.partial(outer_kernel, count=count), out_shape=[p...  5.33 us
    pallas_call x1, Pallas kernels, conv_inner(): pl.pallas_call(inner_kernel, out_shape=[pltpu.VMEM((halves, rows, cols, L...  4.4 us
    ppermute x2, starting transfers between devices, swap_around(): return lax.ppermute(x, 'lon', pairs + [(j, i) for i, j in pairs])  4.07 us
    ppermute x2, starting transfers between devices, swap(): return lax.ppermute(x, 'lat', pairs + [(j, i) for i, j in pairs])  2.3 us
  transfers between devices with their start and end apart: 5, of which 1 were waited for; matrix products, arithmetic and copies ran while one was open for 0% of the time, Pallas kernels for 14%

profile of v3, /device:TPU:0, one launch (start us, length us, event | category | flops | bytes accessed | tf_op | source)
XLA Modules:
  0.0 83.3 jit_solution(15052968228409219748)
XLA Ops:
  0.6 1.3 %edges.1 = (bf16[32,64,256]{2,1,0:T(8,128)(2,1)S(1)}, f32[7,7,256]{2,1,0:T(8,128)S(1)}, bf16[32,8,256]{2,1,0:T(8,128)(2,1)S(1)}, bf16[32,8,256]{2,1,0:T(8,128)(2,1)S(1)}) custom-call(bf16[32,64,256]{2,1,0:T(8,128)(2,1)} %x_ref.1, f32[7,7,256]{2,1,0:T(8,128)} %w_ref.1), custom_call_target="tpu_custom_call" | custom-call | tf_op jit(solution)/shard_map/edges/pallas_call | solution.py:147
  1.9 0.5 collective-permute-start
  2.4 3.6 %collective-permute-start.1 = (bf16[32,8,256]{2,1,0:T(8,128)(2,1)S(1)}, bf16[32,8,256]{2,1,0:T(8,128)(2,1)S(1)}, u32[]{:S(2)}, u32[]{:S(2)}) collective-permute-start(bf16[32,8,256]{2,1,0:T(8,128)(2,1)S(1)} %get-tuple-element.57), channel_id=1, source_target_pairs={{4,8},{12,16},{20,24},{28,0},{8,4},{16,12},{24,20},{0,28},{5,9},{1... | collective-permute-start | bytes 393224 | tf_op jit(solution)/shard_map/ppermute | solution.py:674
  6.0 4.4 %conv_inner.1 = (f32[2,32,64,128]{3,2,1,0:T(8,128)S(1)}, f32[2,119,8,128]{3,2,1,0:T(8,128)S(1)}) custom-call(bf16[32,64,256]{2,1,0:T(8,128)(2,1)S(1)} %get-tuple-element.53.own_ref.atm_ref, f32[7,7,256]{2,1,0:T(8,128)S(1)} %get-tuple-element.54.w_ref), custom_call_target="tpu_custom_call" | custom-call | flops 51380224 | bytes 3145728 | tf_op jit(solution)/shard_map/conv_inner/pallas_call | solution.py:201
  10.4 0.0 collective-permute-done.even_ref.lon_even_ref
  10.4 0.0 collective-permute-done.1.odd_ref.lon_odd_ref
  10.5 1.6 %collective-permute-start.2 = (bf16[3,80,256]{2,1,0:T(8,128)(2,1)S(1)}, bf16[3,80,256]{2,1,0:T(8,128)(2,1)S(1)}, u32[]{:S(2)}, u32[]{:S(2)}) collective-permute-start(bf16[3,80,256]{2,1,0:T(8,128)(2,1)S(1)} %get-tuple-element.60), channel_id=1, source_target_pairs={{0,1},{2,3},{1,0},{3,2},{4,5},{6,7},{5,4},{7,6},{8,9},{10,11},{9,8... | collective-permute-start | bytes 368648 | tf_op jit(solution)/shard_map/ppermute | solution.py:682
  12.1 0.7 collective-permute-start.3
  12.8 0.0 copy-start
  12.8 0.0 copy-start.1
  12.8 0.0 copy-start.2
  12.8 5.3 %conv_outer.1 = (f32[2,32,64,128]{3,2,1,0:T(8,128)S(1)}, bf16[256,1024]{1,0:T(8,128)(2,1)S(1)}, bf16[1024,256]{1,0:T(8,128)(2,1)S(1)}, bf16[256,256]{1,0:T(8,128)(2,1)S(1)}) custom-call(f32[2,32,64,128]{3,2,1,0:T(8,128)S(1)} %get-tuple-element.55.mixed_in.mixed_ref, ...), custom_call_target="tpu_custom_call", output_to_operand_aliasing={{0}: (0, {})} | custom-call | flops 12845056 | bytes 786432 | tf_op jit(solution)/shard_map/conv_outer/pallas_call | solution.py:274
  18.1 0.0 collective-permute-done.2.even_ref
  18.1 0.0 collective-permute-done.3.odd_ref
  18.2 0.0 copy-done
  18.2 0.0 copy-done.1
  18.2 0.0 copy-done.2
  18.2 7.6 %atmosphere.1 = (bf16[32,64,256]{2,1,0:T(8,128)(2,1)}, bf16[32,104,256]{2,1,0:T(8,128)(2,1)}, bf16[32,32,256]{2,1,0:T(8,128)(2,1)}, f32[8,128]{1,0:T(8,128)S(1)}, f32[2,32,64,128]{3,2,1,0:T(8,128)S(1)}) custom-call(s32[32]{0:T(128)S(1)} %bitcast.8, f32[2,32,64,128]{3,2,1,0:T(8,128)S(1)} %get-tuple-element.59.mixed_in, ...), custom_call_target="tpu_custom_call", output_to_operand_aliasing={{4}: (1, {})} | custom-call | flops 2415919104 | bytes 6291456 | tf_op jit(solution)/shard_map/atmosphere/pallas_call | solution.py:496
  25.8 5.4 %all-to-all-start.1 = ((bf16[32,104,256]{2,1,0:T(8,128)(2,1)}), bf16[32,104,256]{2,1,0:T(8,128)(2,1)}, u32[]{:S(2)}, u32[]{:S(2)}) async-start(bf16[32,104,256]{2,1,0:T(8,128)(2,1)} %get-tuple-element.68), calls=%async_computation.1 | async-start | bytes 3407872 | tf_op jit(solution)/shard_map/all_to_all | solution.py:694
  31.2 1.9 %fetch.1 = (bf16[32,128,256]{2,1,0:T(8,128)(2,1)S(1)}, f32[1,256]{1,0:T(1,128)S(1)}, bf16[256,1024]{1,0:T(8,128)(2,1)S(1)}, bf16[1024,256]{1,0:T(8,128)(2,1)S(1)}) custom-call(f32[8,128]{1,0:T(8,128)S(1)} %get-tuple-element.66.mark_ref, bf16[32,128,256]{2,1,0:T(8,128)(2,1)} %bitcast.10, f32[1,256]{1,0:T(1,128)} %bitcast.11, bf16[256,1024]{1,0:T(8,128)(2,1)} %refs_2_.3, ...), custom_call_target="tpu_custom_call" | custom-call | tf_op jit(solution)/shard_map/fetch/pallas_call | solution.py:547
  33.1 38.4 %all-to-all-done.1.packet_hbm = bf16[32,104,256]{2,1,0:T(8,128)(2,1)} async-done(((bf16[32,104,256]{2,1,0:T(8,128)(2,1)}), bf16[32,104,256]{2,1,0:T(8,128)(2,1)}, u32[]{:S(2)}, u32[]{:S(2)}) %all-to-all-start.1) | async-done | bytes 1703968 | tf_op jit(solution)/shard_map/all_to_all | solution.py:694
  71.5 0.0 copy-start.3
  71.5 10.9 %ocean.3 = (bf16[32,128,256]{2,1,0:T(8,128)(2,1)}, f32[1,1]{1,0:T(1,128)}) custom-call(bf16[32,128,256]{2,1,0:T(8,128)(2,1)S(1)} %get-tuple-element.67.state_ref, bf16[32,104,256]{2,1,0:T(8,128)(2,1)} %all-to-all-done.1.packet_hbm, f32[1,256]{1,0:T(1,128)S(1)} %get-tuple-element.69.gain_ref, bf16[256,1024]{1,0:T(8,128)(2,1)S(1)} %get-tuple-element.70.up_ref, ...), custom_call_target="tpu_custom_call" | custom-call | flops 4294967296 | bytes 6291456 | tf_op jit(solution)/shard_map/ocean/pallas_call | solution.py:625
  83.1 0.0 copy-done.3
  (2 shorter events, 0.0 us)
Async XLA Ops:
  1.9 8.5 %collective-permute-start = (bf16[32,8,256]{2,1,0:T(8,128)(2,1)S(1)}, bf16[32,8,256]{2,1,0:T(8,128)(2,1)S(1)}, u32[]{:S(2)}, u32[]{:S(2)}) collective-permute-start(bf16[32,8,256]{2,1,0:T(8,128)(2,1)S(1)} %get-tuple-element.56), channel_id=1, source_target_pairs={{0,4},{8,12},{16,20},{24,28},{4,0},{12,8},{20,16},{28,24},{1,5},{9... | collective-permute-start | bytes 393224 | tf_op jit(solution)/shard_map/ppermute | solution.py:674
  2.4 8.0 %collective-permute-start.1 = (bf16[32,8,256]{2,1,0:T(8,128)(2,1)S(1)}, bf16[32,8,256]{2,1,0:T(8,128)(2,1)S(1)}, u32[]{:S(2)}, u32[]{:S(2)}) collective-permute-start(bf16[32,8,256]{2,1,0:T(8,128)(2,1)S(1)} %get-tuple-element.57), channel_id=1, source_target_pairs={{4,8},{12,16},{20,24},{28,0},{8,4},{16,12},{24,20},{0,28},{5,9},{1... | collective-permute-start | bytes 393224 | tf_op jit(solution)/shard_map/ppermute | solution.py:674
  10.5 7.7 %collective-permute-start.2 = (bf16[3,80,256]{2,1,0:T(8,128)(2,1)S(1)}, bf16[3,80,256]{2,1,0:T(8,128)(2,1)S(1)}, u32[]{:S(2)}, u32[]{:S(2)}) collective-permute-start(bf16[3,80,256]{2,1,0:T(8,128)(2,1)S(1)} %get-tuple-element.60), channel_id=1, source_target_pairs={{0,1},{2,3},{1,0},{3,2},{4,5},{6,7},{5,4},{7,6},{8,9},{10,11},{9,8... | collective-permute-start | bytes 368648 | tf_op jit(solution)/shard_map/ppermute | solution.py:682
  12.1 6.0 %collective-permute-start.3 = (bf16[3,80,256]{2,1,0:T(8,128)(2,1)S(1)}, bf16[3,80,256]{2,1,0:T(8,128)(2,1)S(1)}, u32[]{:S(2)}, u32[]{:S(2)}) collective-permute-start(bf16[3,80,256]{2,1,0:T(8,128)(2,1)S(1)} %get-tuple-element.61), channel_id=1, source_target_pairs={{1,2},{2,1},{5,6},{6,5},{9,10},{10,9},{13,14},{14,13},{17,18},{18,... | collective-permute-start | bytes 368648 | tf_op jit(solution)/shard_map/ppermute | solution.py:682
  12.8 5.4 %copy-start = (s32[32,64]{1,0:T(8,128)S(1)}, s32[32,64]{1,0:T(8,128)}, u32[]{:S(2)}) copy-start(s32[32,64]{1,0:T(8,128)} %mask_ref.1) | copy-start | bytes 24580
  12.8 5.4 %copy-start.1 = (f32[256]{0:T(256)S(1)}, f32[256]{0:T(256)}, u32[]{:S(2)}) copy-start(f32[256]{0:T(256)} %param.16) | copy-start | bytes 3076
  12.8 5.4 %copy-start.2 = (s32[1,1,32]{2,1,0:T(1,128)S(1)}, s32[1,1,32]{2,1,0:T(1,128)}, u32[]{:S(2)}) copy-start(s32[1,1,32]{2,1,0:T(1,128)} %param.21) | copy-start | bytes 388
  25.8 45.8 %all-to-all-start.1 = ((bf16[32,104,256]{2,1,0:T(8,128)(2,1)}), bf16[32,104,256]{2,1,0:T(8,128)(2,1)}, u32[]{:S(2)}, u32[]{:S(2)}) async-start(bf16[32,104,256]{2,1,0:T(8,128)(2,1)} %get-tuple-element.68), calls=%async_computation.1 | async-start | bytes 3407872 | tf_op jit(solution)/shard_map/all_to_all | solution.py:694
  71.5 11.6 %copy-start.3 = (bf16[32,32,256]{2,1,0:T(8,128)(2,1)S(1)}, bf16[32,32,256]{2,1,0:T(8,128)(2,1)}, u32[]{:S(2)}) copy-start(bf16[32,32,256]{2,1,0:T(8,128)(2,1)} %get-tuple-element.74) | copy-start | bytes 1572868
